TPU v7x, 256 devices: a whole 4x4x8 slice. The times are simulated.
256 devices in a mesh: row: 8 (over x, core), col: 32 (over z, y).
Axes of the slice: x: 4, y: 4, z: 8, core: 2. Of those that a mesh axis runs over, the one named last changes fastest.
Arguments:
- source_coords: bfloat16 [32, 524288], P(None, 'row'), may hold values from -6 to 6
- target_coords: bfloat16 [32, 65536], P(None, 'col'), may hold values from -6 to 6
- source_order: int32 [8, 65536], P('row'), may hold values from 0 to 65535, each once within a row
- target_order: int32 [32, 2048], P('col'), may hold values from 0 to 2047, each once within a row
- source_mass: float32 [524288], P('row'), may hold values from -12 to 240
- target_mass: float32 [65536], P('col'), may hold values from -12 to -8
- target_potential: float32 [65536], P('col'), may hold values from -4 to 24
- tile_source: int32 [8, 32, 256], P('row', 'col'), may hold values from 0 to 255, as said below
- tile_target: int32 [8, 32, 256], P('row', 'col'), may hold values from 0 to 7, as said below
- tile_count: int32 [8, 32], P('row', 'col'), may hold values from 64 to 256, as said below
Outputs:
- source_update: float32 [524288], P('row')
- target_update: float32 [65536], P('col')
Inputs may be any that keep to these rules, and one draw needn't show every extreme that they name: Entries k < tile_count[r, c] of an intersection are used; later entries hold valid block numbers and are not part of the support. Within the used entries of an intersection no pair (tile_source, tile_target) repeats. Every source block of a row cluster has a used entry in some intersection of that row cluster. `tile_target`: every target block of a column cluster has a used entry in some intersection of that column cluster. `tile_count`: in every draw some intersection uses all 256 entries.
All inputs are finite; a program needn't handle non-finite values.
Results may differ from a plain program's by a relative error of at most 0.0003.
Values sent between devices are 32-bit elements; how exact they have to be, the bound alone decides.
No kernel may reach another device: no remote copies, remote signals or barrier semaphores. Data moves between devices by JAX's collectives and lax.ppermute only.
A program may use at most 256 MiB of HBM per device.

v0:
```python
import jax
import jax.numpy as jnp
from jax import lax
from jax.sharding import PartitionSpec as P

PC = 32
BLK = 256
SB_DEV = 256
TB_DEV = 8
CAP = 256


epsilon = 0.1
very_negative = -1e30
tile_group = 8


def combined_all(array, axis, combine):
    everything = jax.tree.map(lambda part: lax.all_gather(part, axis), array)
    leading = jax.tree.map(lambda part: part[0], everything)

    def lap(k, so_far):
        return combine(so_far, jax.tree.map(lambda part: part[k], everything))

    return lax.fori_loop(1, lax.axis_size(axis), lap, leading)


def pair_merge(former, latter):
    highest = jnp.maximum(former[0], latter[0])
    return (
        highest,
        former[1] * jnp.exp(former[0] - highest) + latter[1] * jnp.exp(latter[0] - highest),
    )


def tile_costs(source_blocks, source_norm, target_blocks, target_norm, which_source, which_target):
    left_block = jnp.take(source_blocks, which_source, axis=1)
    right_block = jnp.take(target_blocks, which_target, axis=1)
    products = jnp.einsum(
        "dgi,dgj->gij", left_block, right_block, preferred_element_type=jnp.float32
    )
    return (
        source_norm[which_source][:, :, None]
        + target_norm[which_target][:, None, :]
        - 2.0 * products
    ) / PC


def over_tiles(step_fn):
    stacked = lax.map(step_fn, jnp.arange(CAP // tile_group, dtype=jnp.int32))
    return tuple((member.reshape((CAP,) + member.shape[2:]) for member in stacked))


def body(
    source_coords,
    target_coords,
    source_order,
    target_order,
    source_mass,
    target_mass,
    target_potential,
    tile_source,
    tile_target,
    tile_count,
):
    source_blocks = jnp.take(source_coords, source_order[0], axis=1).reshape(PC, SB_DEV, BLK)
    target_blocks = jnp.take(target_coords, target_order[0], axis=1).reshape(PC, TB_DEV, BLK)
    source_norm = jnp.sum(jnp.square(source_blocks.astype(jnp.float32)), axis=0)
    target_norm = jnp.sum(jnp.square(target_blocks.astype(jnp.float32)), axis=0)
    source_weight = jnp.take(source_mass, source_order[0]).reshape(SB_DEV, BLK)
    target_weight = jnp.take(target_mass, target_order[0]).reshape(TB_DEV, BLK)
    start_potential = jnp.take(target_potential, target_order[0]).reshape(TB_DEV, BLK)
    source_list = tile_source[0, 0]
    target_list = tile_target[0, 0]
    filled = tile_count[0, 0]
    slot_index = jnp.arange(CAP, dtype=jnp.int32)

    def group_ids(group_index):
        first_slot = group_index * tile_group
        which_source = lax.dynamic_slice_in_dim(source_list, first_slot, tile_group)
        which_target = lax.dynamic_slice_in_dim(target_list, first_slot, tile_group)
        active_group = lax.dynamic_slice_in_dim(slot_index, first_slot, tile_group) < filled
        return (which_source, which_target, active_group)

    def row_step(group_index):
        which_source, which_target, active_group = group_ids(group_index)
        tile_cost = tile_costs(
            source_blocks, source_norm, target_blocks, target_norm, which_source, which_target
        )
        scores = (start_potential[which_target][:, None, :] - tile_cost) / epsilon
        highest = jnp.max(scores, axis=2)
        summed = jnp.sum(jnp.exp(scores - highest[:, :, None]), axis=2)
        highest = jnp.where(active_group[:, None], highest, very_negative)
        summed = jnp.where(active_group[:, None], summed, 0.0)
        return (highest, summed)

    row_results = over_tiles(row_step)
    tile_max = row_results[0]
    tile_sum = row_results[1]
    row_max = jnp.full((SB_DEV, BLK), very_negative, jnp.float32).at[source_list].max(tile_max)
    row_sum = (
        jnp.zeros((SB_DEV, BLK), jnp.float32)
        .at[source_list]
        .add(tile_sum * jnp.exp(tile_max - row_max[source_list]))
    )
    row_max, row_sum = combined_all((row_max, row_sum), "col", pair_merge)
    source_dual = epsilon * source_weight - epsilon * (row_max + jnp.log(row_sum))

    def col_step(group_index):
        which_source, which_target, active_group = group_ids(group_index)
        tile_cost = tile_costs(
            source_blocks, source_norm, target_blocks, target_norm, which_source, which_target
        )
        scores = (source_dual[which_source][:, :, None] - tile_cost) / epsilon
        highest = jnp.max(scores, axis=1)
        summed = jnp.sum(jnp.exp(scores - highest[:, None, :]), axis=1)
        highest = jnp.where(active_group[:, None], highest, very_negative)
        summed = jnp.where(active_group[:, None], summed, 0.0)
        return (highest, summed)

    col_results = over_tiles(col_step)
    col_tile_max = col_results[0]
    col_tile_sum = col_results[1]
    col_max = jnp.full((TB_DEV, BLK), very_negative, jnp.float32).at[target_list].max(col_tile_max)
    col_sum = (
        jnp.zeros((TB_DEV, BLK), jnp.float32)
        .at[target_list]
        .add(col_tile_sum * jnp.exp(col_tile_max - col_max[target_list]))
    )
    col_max, col_sum = combined_all((col_max, col_sum), "row", pair_merge)
    target_dual = epsilon * target_weight - epsilon * (col_max + jnp.log(col_sum))
    source_update = (
        jnp.zeros((source_order.shape[1],), jnp.float32)
        .at[source_order[0]]
        .set(source_dual.reshape(-1))
    )
    target_update = (
        jnp.zeros((target_order.shape[1],), jnp.float32)
        .at[target_order[0]]
        .set(target_dual.reshape(-1))
    )
    return (source_update, target_update)


def solution(mesh):
    in_specs = (
        P(None, "row"),
        P(None, "col"),
        P("row", None),
        P("col", None),
        P("row"),
        P("col"),
        P("col"),
        P("row", "col", None),
        P("row", "col", None),
        P("row", "col"),
    )
    out_specs = (P("row"), P("col"))
    return jax.shard_map(body, mesh=mesh, in_specs=in_specs, out_specs=out_specs, check_vma=False)
```

profile of v0, /device:TPU:1, one launch (start us, length us, event | category | flops | bytes accessed | tf_op | source)
XLA Modules:
  0.0 1617.4 jit_solution(149249746063002536)
XLA Ops:
  14.7 11.8 gather_fusion.14
  27.2 11.8 gather_fusion.13
  39.0 13.6 copy.20
  52.8 225.7 %gather_fusion.11 = bf16[65536,32]{1,0:T(8,128)(2,1)} fusion(bf16[32,65536]{0,1:T(8,128)(2,1)} %copy.20, s32[65536]{0:T(1024)S(1)} %broadcast_clamp_fusion), kind=kCustom, calls=%fused_computation.13 | custom fusion | bytes 8650752 | tf_op jit(solution)/shard_map/jit(_take)/gather | solution.py:66
  278.4 22.1 %multiply_reduce_fusion = f32[65536]{0:T(1024)S(1)} fusion(bf16[65536,32]{1,0:T(8,128)(2,1)} %gather_fusion.11, pred[65536]{0:T(1024)(128)(4,1)S(1)} %compare_and_fusion.4), kind=kLoop, calls=%fused_computation.75 | loop fusion | flops 8323072 | bytes 4521984 | tf_op jit(solution)/shard_map/reduce_sum | solution.py:68
  300.9 6.2 gather_fusion.12
  307.8 14.3 copy.22
  322.5 4.6 broadcast_select_fusion
  327.2 294.6 %while.58 = (s32[]{:T(128)}, f32[32,8,256]{2,1,0:T(8,128)S(1)}, f32[32,8,256]{2,1,0:T(8,128)S(1)}, s32[32]{0:T(128)S(1)}, s32[256]{0:T(256)S(1)}, /*index=5*/s32...) while((s32[]{:T(128)}, f32[32,8,256]{2,1,0:T(8,128)S(1)}, ...), condition=%wide.region_5.9_spmd, body=%wide.region_2.8_spmd.sunk | while | flops 38406252 | bytes 5121175 | solution.py:50
  329.2 2.7 gather_fusion.1
  338.4 2.7 gather_fusion.1
  366.0 2.7 gather_fusion.1
  384.4 2.7 gather_fusion.1
  402.8 2.7 gather_fusion.1
  421.2 2.7 gather_fusion.1
  448.9 2.7 gather_fusion.1
  624.8 4.6 scatter_custom_fusion.1
  629.4 362.7 %gather_fusion.10 = f32[65536]{0:T(1024)S(1)} fusion(f32[65536]{0:T(1024)S(1)} %copy-done, s32[65536]{0:T(1024)S(1)} %broadcast_clamp_fusion), kind=kCustom, calls=%fused_computation.12 | custom fusion | bytes 786432 | tf_op jit(solution)/shard_map/jit(_take)/gather | solution.py:70
  994.3 39.5 %while.59 = (s32[]{:T(128)}, f32[256,256]{1,0:T(8,128)S(1)}, f32[256,256]{1,0:T(8,128)S(1)}, f32[32,256,256]{2,1,0:T(8,128)}, f32[32,256,256]{2,1,0:T(8,128)}, /*index=5*/s32[]{:T(128)}, s32[]{:T(128)}, s32[]{:T(128)}) while((s32[]{:T(128)}, f32[256,256]{1,0:T(8,128)S(1)}, f32[256,256]{1,0:T(8,128)S(1)}, f32[32,256,256]{2,1,0:T(8,128)}, ...), condition=%wide.region_9.13_spmd, body=%wide.region_8.12_spmd.sunk | while | flops 393221 | bytes 1572995 | solution.py:25
  1034.1 294.6 %while.60 = (s32[]{:T(128)}, f32[32,8,256]{2,1,0:T(8,128)S(1)}, f32[32,8,256]{2,1,0:T(8,128)S(1)}, s32[32]{0:T(128)S(1)}, s32[256]{0:T(256)S(1)}, /*index=5*/s32...) while((s32[]{:T(128)}, f32[32,8,256]{2,1,0:T(8,128)S(1)}, ...), condition=%wide.region_14.18_spmd, body=%wide.region_11.17_spmd.sunk | while | flops 38406252 | bytes 5121175 | solution.py:50
  1330.7 15.8 all-gather.2
  1348.8 12.8 all-gather.3
  1361.8 240.2 %scatter_custom_fusion.2 = f32[65536]{0:T(1024)} fusion(s32[65536]{0:T(1024)S(1)} %bitcast.149, f32[65536]{0:T(1024)S(1)} %bitcast.152, f32[]{:T(128)} %constant.218.clone.1), kind=kCustom, calls=%fused_computation.101 | custom fusion | bytes 262148 | tf_op jit(solution)/shard_map/scatter | solution.py:135
  1602.0 8.6 scatter_custom_fusion.5
  (935 shorter events, 583.1 us)
Async XLA Ops:
  7.2 622.3 %copy-start = (f32[65536]{0:T(1024)S(1)}, f32[65536]{0:T(1024)}, u32[]{:S(2)}) copy-start(f32[65536]{0:T(1024)} %param.28) | copy-start | bytes 786436
  7.2 7.5 copy-start.2
  7.2 985.1 %all-gather.7.cloned.1.call-start = ((), (), s32[]{:S(2)}) async-start(), calls=%async_computation | async-start | bytes 8650752 | tf_op jit(solution)/shard_map/all_gather | solution.py:19
  14.7 11.8 copy-start.6
  26.5 0.7 copy-start.3
  39.0 13.7 copy-start.4
  278.4 22.2 %copy-start.5 = (bf16[32,2048]{1,0:T(8,128)(2,1)S(1)}, bf16[32,2048]{1,0:T(8,128)(2,1)}, u32[]{:S(2)}) copy-start(bf16[32,2048]{1,0:T(8,128)(2,1)} %param.25) | copy-start | bytes 393220
  322.5 4.8 copy-start.7
  322.5 4.8 copy-start.8
  624.5 368.8 %all-gather.9.cloned.1.call-start = ((), (), s32[]{:S(2)}) async-start(), calls=%async_computation.1 | async-start | bytes 8650752 | tf_op jit(solution)/shard_map/all_gather | solution.py:19
  1328.7 281.9 %copy-start.1 = (f32[65536]{0:T(1024)S(1)}, f32[65536]{0:T(1024)}, u32[]{:S(2)}) copy-start(f32[65536]{0:T(1024)} %param.28) | copy-start | bytes 786436
Sparse Core Ops, SparseCore 0:
  624.7 101.8 all-gather.6
  729.2 95.6 all-gather.8
where the time goes:
time: 1620 us
  local copies, waits for them, and re-layouts  1260 us (78%)
  other arithmetic  161 us (10%)
  matrix products  111 us (7%)
  loops' own time  46.2 us (3%)
  blocking collectives  28.6 us (2%)
    gather x2, local copies, waits for them, and re-layouts, body(): source_weight = jnp.take(source_mass, source_order[0]).reshape(SB_DEV, BLK)  363 us
    scatter x1, local copies, waits for them, and re-layouts, body(): source_update = jnp.zeros((source_order.shape[1],), jnp.float32).at[sourc...  240 us
    gather x2, local copies, waits for them, and re-layouts, body(): jnp.take(source_coords, source_order[0], axis=1).reshape(PC, SB_DEV, BLK)  240 us
    gather x64, local copies, waits for them, and re-layouts, tile_costs(): left_block = jnp.take(source_blocks, which_source, axis=1)  176 us
    dot_general x64, matrix products, tile_costs(): jnp.einsum('dgi,dgj->gij', left_block, right_block, preferred_element_typ...  111 us
    lt x64, other arithmetic, group_ids(): lax.dynamic_slice_in_dim(slot_index, first_slot, tile_group) < filled  46.5 us
    another operation x2, loops' own time, over_tiles(): stacked = lax.map(step_fn, jnp.arange(CAP // tile_group, dtype=jnp.int32))  45.4 us
    add x38, other arithmetic, pair_merge(): former[1] * jnp.exp(former[0] - highest)  38.9 us
  transfers between devices with their start and end apart: 2, of which 0 were waited for; matrix products, arithmetic and copies ran while one was open for 23% of the time, Pallas kernels for 0%

commit v1 on v0

v1 whole, which is shorter than its diff:
```python
import functools
import math

import jax
import jax.numpy as jnp
from jax import lax
from jax.experimental import pallas as pl
from jax.experimental.pallas import tpu as pltpu
from jax.sharding import PartitionSpec as P

PC = 32
BLK = 256
Z = 8
Y = 4
ROWS = 8
SRC = 65536
TGT = 2048
CHUNK = SRC // Y
NB = CHUNK // BLK
TB = TGT // BLK
CAP = 256
PACK = 40
LOG2E = math.log2(math.e)
KAPPA = 10.0 * LOG2E
LN2 = math.log(2.0)
LOW = -1e30

f32 = jnp.float32
bf16 = jnp.bfloat16
NT = (((1,), (1,)), ((), ()))


def iota(shape, axis):
    return lax.broadcasted_iota(jnp.int32, shape, axis)


def indicator(condition):
    return jnp.where(condition, 1.0, 0.0).astype(bf16)


def three(value):
    first = value.astype(bf16).astype(f32)
    rest = value - first
    second = rest.astype(bf16).astype(f32)
    return first, second, rest - second


def vmem():
    return pl.BlockSpec(memory_space=pltpu.VMEM)


def smem():
    return pl.BlockSpec(memory_space=pltpu.SMEM)


def call(kernel, name, out_shape, in_specs, scratch, flops=0, nbytes=0, exps=0, limit=48):
    many = isinstance(out_shape, (list, tuple))
    return pl.pallas_call(
        kernel,
        out_shape=out_shape,
        in_specs=in_specs,
        out_specs=[vmem() for _ in out_shape] if many else vmem(),
        scratch_shapes=scratch,
        compiler_params=pltpu.CompilerParams(vmem_limit_bytes=limit * 2**20),
        cost_estimate=pl.CostEstimate(flops=flops, bytes_accessed=nbytes, transcendentals=exps),
        name=name,
    )


def target_kernel(coords, order, potential, which_source, which_target, count, out, left):
    sub8 = iota((8, TGT), 0)
    vh, vm, vl = three(jnp.broadcast_to(potential[...], (8, TGT)))
    part = jnp.where(sub8 == 0, vh, jnp.where(sub8 == 1, vm, jnp.where(sub8 == 2, vl, 0.0)))
    left[0:32, :] = coords[...]
    left[32:48, :] = jnp.concatenate([part, jnp.zeros((8, TGT), f32)], axis=0).astype(bf16)
    number = iota((TGT, BLK), 0)

    def one_block(b, carry):
        span = pl.ds(pl.multiple_of(b * BLK, BLK), BLK)
        picked = indicator(number == order[:, span])
        got = jnp.dot(left[...], picked, preferred_element_type=f32)
        y = got[0:32]
        v = got[32:33] + got[33:34] + got[34:35]
        a = (v - jnp.sum(y * y, axis=0, keepdims=True) * (1.0 / PC)) * KAPPA
        out[0:32, span] = y
        out[32:40, span] = jnp.broadcast_to(a, (8, BLK))
        return carry

    lax.fori_loop(0, TB, one_block, 0)

    src = which_source[...]
    used = iota((1, CAP), 1) < count[0, 0]
    quarter = jnp.where(used, src // NB, 7)
    member = jnp.where(iota((8, CAP), 0) == quarter, 1.0, 0.0)
    earlier = indicator(iota((CAP, CAP), 0) < iota((CAP, CAP), 1))
    before = jnp.dot(member.astype(bf16), earlier, preferred_element_type=f32)
    rank = jnp.sum(member * before, axis=0, keepdims=True).astype(jnp.int32)
    place = quarter * CAP + rank
    sub16 = iota((16, CAP), 0)
    code = jnp.where(
        sub16 == 0,
        ((src % NB) * 8).astype(f32),
        jnp.where(sub16 == 1, (which_target[...] + 1).astype(f32), 0.0),
    ).astype(bf16)
    chosen = indicator(iota((Y * CAP, CAP), 0) == place)
    listed = lax.dot_general(code, chosen, NT, preferred_element_type=f32)
    out[39:40, 0 : Y * CAP] = listed[0:1] + listed[1:2]
    out[39:40, Y * CAP :] = jnp.zeros((1, TGT - Y * CAP), f32)


def gather_kernel(coords, mass, order, out, table, rows):
    sub8 = iota((8, 128), 0)
    lane = lax.rem(sub8, 4)
    tail = jnp.concatenate([jnp.where(sub8 == 0, 1.0, 0.0), jnp.zeros((16, 128), f32)], axis=0)

    def build(b):
        span = pl.ds(pl.multiple_of(b * 128, 128), 128)
        x = coords[:, span].astype(f32)
        norm = jnp.sum(x * x, axis=0, keepdims=True) * (-KAPPA / PC)
        weight = mass[pl.ds(b, 1), :] * LOG2E
        both = jnp.where(sub8 < 4, jnp.broadcast_to(norm, (8, 128)), jnp.broadcast_to(weight, (8, 128)))
        h, m, l = three(both)
        part = jnp.where(lane == 0, h, jnp.where(lane == 1, m, jnp.where(lane == 2, l, 1.0)))
        table[span, :] = jnp.concatenate([x, x, x, part, tail], axis=0).T

    def build_four(g, carry):
        for u in range(4):
            build(g * 4 + u)
        return carry

    lax.fori_loop(0, SRC // 512, build_four, 0)

    def one_block(b, carry):
        base = b * BLK
        for i in range(BLK):
            rows[pl.ds(i, 1), :] = table[pl.ds(order[0, base + i], 1), :]
        out[pl.ds(pl.multiple_of(base, BLK), BLK), :] = rows[...].astype(bf16)
        return carry

    lax.fori_loop(0, NB, one_block, 0)


def tiles(left_of, right_of, slot_of, highest, total, counts, codes):
    def tile(d, e):
        code = codes[d, e]
        s, t = code // 8, lax.rem(code, 8)
        score = lax.dot_general(left_of(d, s, t), right_of(d, s, t), NT, preferred_element_type=f32)
        top = jnp.max(score, axis=0, keepdims=True)
        return slot_of(d, s, t), top, jnp.sum(jnp.exp2(score - top), axis=0, keepdims=True)

    def add(slot, top, summed):
        for half in range(2):
            here, there = pl.ds(2 * slot + half, 1), slice(half * 128, half * 128 + 128)
            old = highest[here, :]
            new = jnp.maximum(old, top[:, there])
            total[here, :] = total[here, :] * jnp.exp2(old - new) + summed[:, there] * jnp.exp2(top[:, there] - new)
            highest[here, :] = new

    highest[...] = jnp.full(highest.shape, LOW, f32)
    total[...] = jnp.zeros(total.shape, f32)
    for d in range(Y):
        count = counts[d]

        def pair(g, carry):
            first = tile(d, 2 * g)
            has = 2 * g + 1 < count
            slot, top, summed = tile(d, jnp.where(has, 2 * g + 1, 2 * g))
            add(*first)
            add(slot, jnp.where(has, top, LOW), jnp.where(has, summed, 0.0))
            return carry

        lax.fori_loop(0, (count + 1) // 2, pair, 0)
    return jnp.where(total[...] > 0.0, highest[...] + jnp.log2(total[...]), LOW)


def row_kernel(source, p0, p1, p2, p3, codes, counts, partial, late, early, highest, total):
    lane = iota((128, 128), 1)
    turned = ((lane >= 100) & (lane <= 102)) | ((lane >= 105) & (lane <= 107))
    sub8 = iota((8, 128), 0)
    for d, pack in enumerate((p0, p1, p2, p3)):

        def build(b, carry):
            span = pl.ds(pl.multiple_of(b * 128, 128), 128)
            h, m, l = three(pack[0:32, span] * (KAPPA / 16.0))
            ah, am, al = three(jnp.broadcast_to(pack[32:33, span], (8, 128)))
            part = jnp.where(sub8 < 3, 1.0, jnp.where(sub8 == 3, ah, jnp.where(sub8 == 7, am, 0.0)))
            last = jnp.where(sub8 == 0, al, 0.0)
            rows = jnp.concatenate([h, m, l, part, last, jnp.zeros((16, 128), f32)], axis=0).T
            place = pl.ds(pl.multiple_of(d * TGT + b * 128, 128), 128)
            early[place, :] = rows.astype(bf16)
            late[place, :] = jnp.where(turned, 1.0, rows).astype(bf16)
            return carry

        lax.fori_loop(0, TGT // 128, build, 0)

    partial[...] = tiles(
        lambda d, s, t: early[pl.ds(pl.multiple_of(d * TGT + t * BLK, BLK), BLK), :],
        lambda d, s, t: source[pl.ds(pl.multiple_of(s * BLK, BLK), BLK), :],
        lambda d, s, t: s,
        highest,
        total,
        counts,
        codes,
    )


def merged(parts):
    top = functools.reduce(jnp.maximum, parts)
    return top + jnp.log2(sum(jnp.exp2(part - top) for part in parts))


def merge_kernel(*refs):
    refs[-1][...] = merged([ref[...] for ref in refs[:-1]])


def col_kernel(source, late, lse, codes, counts, partial, filled, highest, total):
    sub8 = iota((8, 128), 0)

    def fill(b, carry):
        for half in range(2):
            row = -lse[pl.ds(2 * b + half, 1), :]
            h, m, l = three(jnp.broadcast_to(row, (8, 128)))
            part = jnp.where(sub8 == 1, h, jnp.where(sub8 == 2, m, jnp.where(sub8 == 3, l, 0.0)))
            rows = jnp.concatenate([jnp.zeros((104, 128), f32), part, jnp.zeros((16, 128), f32)], axis=0).T
            span = pl.ds(pl.multiple_of(b * BLK + half * 128, 128), 128)
            filled[span, :] = source[span, :] + rows.astype(bf16)
        return carry

    lax.fori_loop(0, NB, fill, 0)
    partial[...] = tiles(
        lambda d, s, t: filled[pl.ds(pl.multiple_of(s * BLK, BLK), BLK), :],
        lambda d, s, t: late[pl.ds(pl.multiple_of(d * TGT + t * BLK, BLK), BLK), :],
        lambda d, s, t: d * TB + t,
        highest,
        total,
        counts,
        codes,
    )


def flat(block):
    return jnp.concatenate([block[u : u + 1, :] for u in range(8)], axis=1)


def spread(order_row, value_row, high_rows):
    n = order_row.shape[1]
    high = indicator(iota((high_rows, n), 0) == order_row // 128)
    match = iota((128, n), 0) == lax.rem(order_row, 128)
    first = value_row.astype(bf16).astype(f32)
    low = jnp.concatenate(
        [jnp.where(match, first, 0.0), jnp.where(match, value_row - first, 0.0)], axis=0
    ).astype(bf16)
    return lax.dot_general(high, low, NT, preferred_element_type=f32)


def source_kernel(order, l0, l1, l2, l3, chunks, mass, out, total):
    total[...] = jnp.zeros(total.shape, f32)
    for d, lse in enumerate((l0, l1, l2, l3)):
        first = chunks[d] * (2 * NB)

        def step(g, carry):
            where = order[pl.ds(pl.multiple_of(first + g * 8, 8), 8), :]
            value = lse[pl.ds(pl.multiple_of(g * 8, 8), 8), :]
            total[...] += spread(flat(where), flat(value), SRC // 128)
            return carry

        lax.fori_loop(0, NB // 4, step, 0)
    out[...] = 0.1 * mass[...] - (0.1 * LN2) * (total[:, 0:128] + total[:, 128:256])


def final_kernel(*refs):
    order, mass, potential, out = refs[8:12]
    lse = merged([ref[...] for ref in refs[:8]])
    total = jnp.zeros((TGT // 128, 256), f32)
    for g in range(TGT // 1024):
        total += spread(flat(order[g * 8 : g * 8 + 8, :]), flat(lse[g * 8 : g * 8 + 8, :]), TGT // 128)
    out[...] = 0.1 * mass[...] + potential[...] - (0.1 * LN2) * (total[:, 0:128] + total[:, 128:256])


def y_shift(d):
    return [(z * Y + y, z * Y + (y + d) % Y) for z in range(Z) for y in range(Y)]


def z_shift(d):
    return [(z * Y + y, (z + d) % Z * Y + y) for z in range(Z) for y in range(Y)]


def row_shift(d):
    return [(r, (r + d) % ROWS) for r in range(ROWS)]


def body(
    source_coords,
    target_coords,
    source_order,
    target_order,
    source_mass,
    target_mass,
    target_potential,
    tile_source,
    tile_target,
    tile_count,
):
    shape = jax.ShapeDtypeStruct
    y = lax.rem(lax.axis_index("col"), Y)
    mass = source_mass.reshape(SRC // 128, 128)

    pack = call(
        target_kernel,
        "target_gather",
        shape((PACK, TGT), f32),
        [vmem()] * 5 + [smem()],
        [pltpu.VMEM((48, TGT), bf16)],
        flops=2 * 48 * TGT * TGT,
    )(
        target_coords,
        target_order,
        target_potential.reshape(1, TGT),
        tile_source.reshape(1, CAP),
        tile_target.reshape(1, CAP),
        tile_count,
    )
    packs = [pack] + [lax.ppermute(pack, "col", y_shift(d)) for d in range(1, Y)]

    source = call(
        gather_kernel,
        "source_gather",
        shape((CHUNK, 128), bf16),
        [vmem(), vmem(), smem()],
        [pltpu.VMEM((SRC, 128), f32), pltpu.VMEM((BLK, 128), f32)],
        flops=2 * 10**10,
        nbytes=64 * 2**20,
        limit=56,
    )(source_coords, mass, lax.dynamic_slice(source_order, (0, y * CHUNK), (1, CHUNK)))

    lists = jnp.concatenate([lax.dynamic_slice(p, (PACK - 1, y * CAP), (1, CAP)) for p in packs], axis=0)
    codes = lists.astype(jnp.int32) - 1
    counts = jnp.sum((lists > 0.5).astype(jnp.int32), axis=1)

    partial, late = call(
        row_kernel,
        "row_pass",
        [shape((2 * NB, 128), f32), shape((Y * TGT, 128), bf16)],
        [vmem()] * 5 + [smem()] * 2,
        [pltpu.VMEM((Y * TGT, 128), bf16), pltpu.VMEM((2 * NB, 128), f32), pltpu.VMEM((2 * NB, 128), f32)],
    )(source, *packs, codes, counts)

    partials = [partial] + [lax.ppermute(partial, "col", z_shift(d)) for d in range(1, Z)]
    lse = call(merge_kernel, "row_merge", shape((2 * NB, 128), f32), [vmem()] * Z, [])(*partials)
    lses = [lse] + [lax.ppermute(lse, "col", y_shift(d)) for d in range(1, Y)]

    target_partial = call(
        col_kernel,
        "col_pass",
        shape((2 * Y * TB, 128), f32),
        [vmem()] * 3 + [smem()] * 2,
        [
            pltpu.VMEM((CHUNK, 128), bf16),
            pltpu.VMEM((2 * Y * TB, 128), f32),
            pltpu.VMEM((2 * Y * TB, 128), f32),
        ],
        flops=2 * 10**10,
        exps=10**7,
    )(source, late, lse, codes, counts)

    own = [target_partial[0 : 2 * TB]] + [
        lax.ppermute(target_partial[2 * d * TB : 2 * (d + 1) * TB], "col", y_shift(-d)) for d in range(1, Y)
    ]
    own = call(merge_kernel, "col_merge", shape((2 * TB, 128), f32), [vmem()] * Y, [])(*own)
    all_rows = [own] + [lax.ppermute(own, "row", row_shift(d)) for d in range(1, ROWS)]

    chunks = lax.rem(y + Y - jnp.arange(Y, dtype=jnp.int32), Y)
    source_update = call(
        source_kernel,
        "source_scatter",
        shape((SRC // 128, 128), f32),
        [vmem()] * 5 + [smem(), vmem()],
        [pltpu.VMEM((SRC // 128, 256), f32)],
        flops=2 * 512 * 256 * SRC,
        nbytes=2**20,
    )(source_order.reshape(SRC // 128, 128), *lses, chunks, mass)

    target_update = call(
        final_kernel,
        "target_scatter",
        shape((TGT // 128, 128), f32),
        [vmem()] * 11,
        [],
    )(
        *all_rows,
        target_order.reshape(TGT // 128, 128),
        target_mass.reshape(TGT // 128, 128),
        target_potential.reshape(TGT // 128, 128),
    )
    return (source_update.reshape(SRC), target_update.reshape(TGT))


def solution(mesh):
    in_specs = (
        P(None, "row"),
        P(None, "col"),
        P("row", None),
        P("col", None),
        P("row"),
        P("col"),
        P("col"),
        P("row", "col", None),
        P("row", "col", None),
        P("row", "col"),
    )
    out_specs = (P("row"), P("col"))
    return jax.shard_map(body, mesh=mesh, in_specs=in_specs, out_specs=out_specs, check_vma=False)
```

time: 1620 us -> 194 us (0.12)
  the two profiles are of different devices: /device:TPU:1 before, /device:TPU:40 now
where the time goes in v1:
time: 194 us
  Pallas kernels  128 us (66%)
  starting transfers between devices  44.8 us (23%)
  waiting for transfers between devices  13.7 us (7%)
  local copies, waits for them, and re-layouts  5.46 us (3%)
    pallas_call x1, Pallas kernels, body(): call(gather_kernel, 'source_gather', shape((CHUNK, 128), bf16), [vmem(),...  35.6 us
    pallas_call x1, Pallas kernels, body(): call(source_kernel, 'source_scatter', shape((SRC // 128, 128), f32), [vme...  33.9 us
    pallas_call x1, Pallas kernels, body(): call(row_kernel, 'row_pass', [shape((2 * NB, 128), f32), shape((Y * TGT,...  27.5 us
    pallas_call x1, Pallas kernels, body(): call(col_kernel, 'col_pass', shape((2 * Y * TB, 128), f32), [vmem()] * 3...  26.9 us
    ppermute x7, starting transfers between devices, body(): lax.ppermute(partial, 'col', z_shift(d))  17 us
    ppermute x7, starting transfers between devices, body(): lax.ppermute(own, 'row', row_shift(d))  12.6 us
    ppermute x7, waiting for transfers between devices, body(): lax.ppermute(partial, 'col', z_shift(d))  8.04 us
    ppermute x3, starting transfers between devices, body(): lses = [lse] + [lax.ppermute(lse, 'col', y_shift(d)) for d in range(1, Y)]  5.59 us
  transfers between devices with their start and end apart: 23, of which 8 were waited for; matrix products, arithmetic and copies ran while one was open for 1% of the time, Pallas kernels for 19%

profile of v1, /device:TPU:40, one launch (start us, length us, event | category | flops | bytes accessed | tf_op | source)
XLA Modules:
  0.0 193.6 jit_solution(7337840296595529195)
XLA Ops:
  4.9 2.9 %target_gather.1.p0 = f32[40,2048]{1,0:T(8,128)S(1)} custom-call(bf16[32,2048]{1,0:T(8,128)(2,1)S(1)} %copy-done.7, s32[1,2048]{1,0:T(1,128)S(1)} %copy-done.1, f32[1,2048]{1,0:T(1,128)S(1)} %bitcast.12, s32[1,256]{1,0:T(1,128)S(1)} %bitcast.17, s32[1,256]{1,0:T(1,128)S(1)} %bitcast.18, s32[1,1]{1,0:T(1,128)S(6)} %copy.12.count), custom_call_target="tpu_custom_call" | custom-call | flops 402653184 | tf_op jit(solution)/shard_map/target_gather/pallas_call | solution.py:308
  8.3 2.6 %collective-permute-start.1 = (f32[40,2048]{1,0:T(8,128)S(1)}, f32[40,2048]{1,0:T(8,128)S(1)}, u32[]{:S(2)}, u32[]{:S(2)}) collective-permute-start(f32[40,2048]{1,0:T(8,128)S(1)} %target_gather.1.p0), channel_id=1, source_target_pairs={{0,2},{1,3},{2,0},{3,1},{4,6},{5,7},{6,4},{7,5},{8,10},{9,11},{10,... | collective-permute-start | bytes 983048 | tf_op jit(solution)/shard_map/ppermute | solution.py:323
  10.9 1.9 collective-permute-start
  12.8 1.5 constant_dynamic-slice_fusion.4.order
  14.3 35.6 %source_gather.1.source = bf16[16384,128]{1,0:T(8,128)(2,1)} custom-call(bf16[32,65536]{1,0:T(8,128)(2,1)} %coords.2, f32[512,128]{1,0:T(8,128)} %bitcast.15, s32[1,16384]{1,0:T(1,128)} %constant_dynamic-slice_fusion.4.order), custom_call_target="tpu_custom_call" | custom-call | flops 20000000000 | bytes 67108864 | tf_op jit(solution)/shard_map/source_gather/pallas_call | solution.py:325
  50.3 27.5 %row_pass.1 = (f32[128,128]{1,0:T(8,128)S(1)}, bf16[8192,128]{1,0:T(8,128)(2,1)S(1)}) custom-call(bf16[16384,128]{1,0:T(8,128)(2,1)} %source_gather.1.source, f32[40,2048]{1,0:T(8,128)S(1)} %target_gather.1.p0, f32[40,2048]{1,0:T(8,128)S(1)} %collective-permute-done.p1, f32[40,2048]{1,0:T(8,128)S(1)} %collective-permute-done.1.p2, ...), custom_call_target="tpu_custom_call" | custom-call | tf_op jit(solution)/shard_map/row_pass/pallas_call | solution.py:340
  77.9 5.7 %collective-permute-start.8 = (f32[128,128]{1,0:T(8,128)S(1)}, f32[128,128]{1,0:T(8,128)S(1)}, u32[]{:S(2)}, u32[]{:S(2)}) collective-permute-start(f32[128,128]{1,0:T(8,128)S(1)} %get-tuple-element.4.refs_0_), channel_id=1, source_target_pairs={{0,24},{1,25},{2,26},{3,27},{4,28},{5,29},{6,30},{7,31},{8,0},{9,1... | collective-permute-start | bytes 196616 | tf_op jit(solution)/shard_map/ppermute | solution.py:348
  83.6 3.4 %collective-permute-start.7 = (f32[128,128]{1,0:T(8,128)S(1)}, f32[128,128]{1,0:T(8,128)S(1)}, u32[]{:S(2)}, u32[]{:S(2)}) collective-permute-start(f32[128,128]{1,0:T(8,128)S(1)} %get-tuple-element.4.refs_0_), channel_id=1, source_target_pairs={{0,20},{1,21},{2,22},{3,23},{4,24},{5,25},{6,26},{7,27},{8,28},{9,... | collective-permute-start | bytes 196616 | tf_op jit(solution)/shard_map/ppermute | solution.py:348
  87.0 4.9 %collective-permute-start.5 = (f32[128,128]{1,0:T(8,128)S(1)}, f32[128,128]{1,0:T(8,128)S(1)}, u32[]{:S(2)}, u32[]{:S(2)}) collective-permute-start(f32[128,128]{1,0:T(8,128)S(1)} %get-tuple-element.4.refs_0_), channel_id=1, source_target_pairs={{0,12},{1,13},{2,14},{3,15},{4,16},{5,17},{6,18},{7,19},{8,20},{9,... | collective-permute-start | bytes 196616 | tf_op jit(solution)/shard_map/ppermute | solution.py:348
  91.9 2.9 %collective-permute-start.4 = (f32[128,128]{1,0:T(8,128)S(1)}, f32[128,128]{1,0:T(8,128)S(1)}, u32[]{:S(2)}, u32[]{:S(2)}) collective-permute-start(f32[128,128]{1,0:T(8,128)S(1)} %get-tuple-element.4.refs_0_), channel_id=1, source_target_pairs={{0,8},{1,9},{2,10},{3,11},{4,12},{5,13},{6,14},{7,15},{8,16},{9,17... | collective-permute-start | bytes 196616 | tf_op jit(solution)/shard_map/ppermute | solution.py:348
  94.9 1.2 collective-permute-done.6.refs_4_
  96.1 4.9 %collective-permute-done.5.refs_3_ = f32[128,128]{1,0:T(8,128)S(1)} collective-permute-done((f32[128,128]{1,0:T(8,128)S(1)}, f32[128,128]{1,0:T(8,128)S(1)}, u32[]{:S(2)}, u32[]{:S(2)}) %collective-permute-start.5) | collective-permute-done | bytes 65568 | tf_op jit(solution)/shard_map/ppermute | solution.py:348
  101.0 1.8 collective-permute-done.4.refs_2_
  103.1 26.9 %col_pass.1 = f32[64,128]{1,0:T(8,128)S(1)} custom-call(bf16[16384,128]{1,0:T(8,128)(2,1)} %source_gather.1.source, bf16[8192,128]{1,0:T(8,128)(2,1)S(1)} %get-tuple-element.5.late, f32[128,128]{1,0:T(8,128)S(1)} %row_merge.1.l0.lse, s32[4,256]{1,0:T(4,128)S(1)} %get-tuple-element.11.codes, s32[4]{0:T(128)S(1)} %get-tuple-element.10.counts), custom_call_target="tpu_custom_call" | custom-call | flops 20000000000 | tf_op jit(solution)/shard_map/col_pass/pallas_call | solution.py:352
  130.1 2.0 %collective-permute-start.14 = (f32[16,128]{1,0:T(8,128)S(1)}, f32[16,128]{1,0:T(8,128)S(1)}, u32[]{:S(2)}, u32[]{:S(2)}) collective-permute-start(f32[16,128]{1,0:T(8,128)S(1)} %get-tuple-element.7), channel_id=1, source_target_pairs={{0,2},{1,3},{2,0},{3,1},{4,6},{5,7},{6,4},{7,5},{8,10},{9,11},{10,... | collective-permute-start | bytes 24584 | tf_op jit(solution)/shard_map/ppermute | solution.py:367
  132.1 2.5 %collective-permute-start.13 = (f32[16,128]{1,0:T(8,128)S(1)}, f32[16,128]{1,0:T(8,128)S(1)}, u32[]{:S(2)}, u32[]{:S(2)}) collective-permute-start(f32[16,128]{1,0:T(8,128)S(1)} %get-tuple-element.8), channel_id=1, source_target_pairs={{0,3},{1,0},{2,1},{3,2},{4,7},{5,4},{6,5},{7,6},{8,11},{9,8},{10,9... | collective-permute-start | bytes 24584 | tf_op jit(solution)/shard_map/ppermute | solution.py:367
  136.1 2.4 %collective-permute-start.21 = (f32[16,128]{1,0:T(8,128)S(1)}, f32[16,128]{1,0:T(8,128)S(1)}, u32[]{:S(2)}, u32[]{:S(2)}) collective-permute-start(f32[16,128]{1,0:T(8,128)S(1)} %col_merge.1.refs_0_), channel_id=1, source_target_pairs={{0,192},{32,224},{64,0},{96,32},{128,64},{160,96},{192,128},{224,1... | collective-permute-start | bytes 24584 | tf_op jit(solution)/shard_map/ppermute | solution.py:370
  138.4 6.6 %collective-permute-start.20 = (f32[16,128]{1,0:T(8,128)S(1)}, f32[16,128]{1,0:T(8,128)S(1)}, u32[]{:S(2)}, u32[]{:S(2)}) collective-permute-start(f32[16,128]{1,0:T(8,128)S(1)} %col_merge.1.refs_0_), channel_id=1, source_target_pairs={{0,160},{32,192},{64,224},{96,0},{128,32},{160,64},{192,96},{224,1... | collective-permute-start | bytes 24584 | tf_op jit(solution)/shard_map/ppermute | solution.py:370
  147.0 2.1 %collective-permute-start.11 = (f32[128,128]{1,0:T(8,128)S(1)}, f32[128,128]{1,0:T(8,128)S(1)}, u32[]{:S(2)}, u32[]{:S(2)}) collective-permute-start(f32[128,128]{1,0:T(8,128)S(1)} %row_merge.1.l0.lse), channel_id=1, source_target_pairs={{0,2},{1,3},{2,0},{3,1},{4,6},{5,7},{6,4},{7,5},{8,10},{9,11},{10,... | collective-permute-start | bytes 196616 | tf_op jit(solution)/shard_map/ppermute | solution.py:350
  149.1 2.5 %collective-permute-start.10 = (f32[128,128]{1,0:T(8,128)S(1)}, f32[128,128]{1,0:T(8,128)S(1)}, u32[]{:S(2)}, u32[]{:S(2)}) collective-permute-start(f32[128,128]{1,0:T(8,128)S(1)} %row_merge.1.l0.lse), channel_id=1, source_target_pairs={{0,1},{1,2},{2,3},{3,0},{4,5},{5,6},{6,7},{7,4},{8,9},{9,10},{10,1... | collective-permute-start | bytes 196616 | tf_op jit(solution)/shard_map/ppermute | solution.py:350
  151.7 2.6 %collective-permute-start.17 = (f32[16,128]{1,0:T(8,128)S(1)}, f32[16,128]{1,0:T(8,128)S(1)}, u32[]{:S(2)}, u32[]{:S(2)}) collective-permute-start(f32[16,128]{1,0:T(8,128)S(1)} %col_merge.1.refs_0_), channel_id=1, source_target_pairs={{0,64},{32,96},{64,128},{96,160},{128,192},{160,224},{192,0},{224,... | collective-permute-start | bytes 24584 | tf_op jit(solution)/shard_map/ppermute | solution.py:370
  154.3 2.2 %collective-permute-done.17.refs_2_ = f32[16,128]{1,0:T(8,128)S(1)} collective-permute-done((f32[16,128]{1,0:T(8,128)S(1)}, f32[16,128]{1,0:T(8,128)S(1)}, u32[]{:S(2)}, u32[]{:S(2)}) %collective-permute-start.17) | collective-permute-done | bytes 8224 | tf_op jit(solution)/shard_map/ppermute | solution.py:370
  156.5 2.0 %collective-permute-done.16.refs_1_ = f32[16,128]{1,0:T(8,128)S(1)} collective-permute-done((f32[16,128]{1,0:T(8,128)S(1)}, f32[16,128]{1,0:T(8,128)S(1)}, u32[]{:S(2)}, u32[]{:S(2)}) %collective-permute-start.16) | collective-permute-done | bytes 8224 | tf_op jit(solution)/shard_map/ppermute | solution.py:370
  159.7 33.9 %source_scatter.1 = f32[512,128]{1,0:T(8,128)} custom-call(s32[512,128]{1,0:T(8,128)S(1)} %bitcast.10, f32[128,128]{1,0:T(8,128)S(1)} %row_merge.1.l0.lse, f32[128,128]{1,0:T(8,128)S(1)} %collective-permute-done.10.l1, f32[128,128]{1,0:T(8,128)S(1)} %collective-permute-done.11.l2, f32[128,128]{1,0:T(8,128)S(1)} %collective-permute-done.12.l3, ...), custom_call_target="tpu_custom_call" | custom-call | flops 17179869184 | bytes 1048576 | tf_op jit(solution)/shard_map/source_scatter/pallas_call | solution.py:373
  (58 shorter events, 9.5 us)
Async XLA Ops:
  7.8 42.2 %collective-permute-start.2 = (f32[40,2048]{1,0:T(8,128)S(1)}, f32[40,2048]{1,0:T(8,128)S(1)}, u32[]{:S(2)}, u32[]{:S(2)}) collective-permute-start(f32[40,2048]{1,0:T(8,128)S(1)} %target_gather.1.p0), channel_id=1, source_target_pairs={{0,3},{1,0},{2,1},{3,2},{4,7},{5,4},{6,5},{7,6},{8,11},{9,8},{10,9... | collective-permute-start | bytes 983048 | tf_op jit(solution)/shard_map/ppermute | solution.py:323
  8.3 41.8 %collective-permute-start.1 = (f32[40,2048]{1,0:T(8,128)S(1)}, f32[40,2048]{1,0:T(8,128)S(1)}, u32[]{:S(2)}, u32[]{:S(2)}) collective-permute-start(f32[40,2048]{1,0:T(8,128)S(1)} %target_gather.1.p0), channel_id=1, source_target_pairs={{0,2},{1,3},{2,0},{3,1},{4,6},{5,7},{6,4},{7,5},{8,10},{9,11},{10,... | collective-permute-start | bytes 983048 | tf_op jit(solution)/shard_map/ppermute | solution.py:323
  10.9 39.2 %collective-permute-start = (f32[40,2048]{1,0:T(8,128)S(1)}, f32[40,2048]{1,0:T(8,128)S(1)}, u32[]{:S(2)}, u32[]{:S(2)}) collective-permute-start(f32[40,2048]{1,0:T(8,128)S(1)} %target_gather.1.p0), channel_id=1, source_target_pairs={{0,1},{1,2},{2,3},{3,0},{4,5},{5,6},{6,7},{7,4},{8,9},{9,10},{10,1... | collective-permute-start | bytes 983048 | tf_op jit(solution)/shard_map/ppermute | solution.py:323
  77.8 14.1 %collective-permute-start.9 = (f32[128,128]{1,0:T(8,128)S(1)}, f32[128,128]{1,0:T(8,128)S(1)}, u32[]{:S(2)}, u32[]{:S(2)}) collective-permute-start(f32[128,128]{1,0:T(8,128)S(1)} %get-tuple-element.4.refs_0_), channel_id=1, source_target_pairs={{0,28},{1,29},{2,30},{3,31},{4,0},{5,1},{6,2},{7,3},{8,4},{9,5},{1... | collective-permute-start | bytes 196616 | tf_op jit(solution)/shard_map/ppermute | solution.py:348
  77.9 17.0 %collective-permute-start.8 = (f32[128,128]{1,0:T(8,128)S(1)}, f32[128,128]{1,0:T(8,128)S(1)}, u32[]{:S(2)}, u32[]{:S(2)}) collective-permute-start(f32[128,128]{1,0:T(8,128)S(1)} %get-tuple-element.4.refs_0_), channel_id=1, source_target_pairs={{0,24},{1,25},{2,26},{3,27},{4,28},{5,29},{6,30},{7,31},{8,0},{9,1... | collective-permute-start | bytes 196616 | tf_op jit(solution)/shard_map/ppermute | solution.py:348
  83.6 11.3 %collective-permute-start.7 = (f32[128,128]{1,0:T(8,128)S(1)}, f32[128,128]{1,0:T(8,128)S(1)}, u32[]{:S(2)}, u32[]{:S(2)}) collective-permute-start(f32[128,128]{1,0:T(8,128)S(1)} %get-tuple-element.4.refs_0_), channel_id=1, source_target_pairs={{0,20},{1,21},{2,22},{3,23},{4,24},{5,25},{6,26},{7,27},{8,28},{9,... | collective-permute-start | bytes 196616 | tf_op jit(solution)/shard_map/ppermute | solution.py:348
  87.0 9.1 %collective-permute-start.6 = (f32[128,128]{1,0:T(8,128)S(1)}, f32[128,128]{1,0:T(8,128)S(1)}, u32[]{:S(2)}, u32[]{:S(2)}) collective-permute-start(f32[128,128]{1,0:T(8,128)S(1)} %get-tuple-element.4.refs_0_), channel_id=1, source_target_pairs={{0,16},{1,17},{2,18},{3,19},{4,20},{5,21},{6,22},{7,23},{8,24},{9,... | collective-permute-start | bytes 196616 | tf_op jit(solution)/shard_map/ppermute | solution.py:348
  87.0 14.0 %collective-permute-start.5 = (f32[128,128]{1,0:T(8,128)S(1)}, f32[128,128]{1,0:T(8,128)S(1)}, u32[]{:S(2)}, u32[]{:S(2)}) collective-permute-start(f32[128,128]{1,0:T(8,128)S(1)} %get-tuple-element.4.refs_0_), channel_id=1, source_target_pairs={{0,12},{1,13},{2,14},{3,15},{4,16},{5,17},{6,18},{7,19},{8,20},{9,... | collective-permute-start | bytes 196616 | tf_op jit(solution)/shard_map/ppermute | solution.py:348
  91.9 10.9 %collective-permute-start.4 = (f32[128,128]{1,0:T(8,128)S(1)}, f32[128,128]{1,0:T(8,128)S(1)}, u32[]{:S(2)}, u32[]{:S(2)}) collective-permute-start(f32[128,128]{1,0:T(8,128)S(1)} %get-tuple-element.4.refs_0_), channel_id=1, source_target_pairs={{0,8},{1,9},{2,10},{3,11},{4,12},{5,13},{6,14},{7,15},{8,16},{9,17... | collective-permute-start | bytes 196616 | tf_op jit(solution)/shard_map/ppermute | solution.py:348
  94.9 8.0 %collective-permute-start.3 = (f32[128,128]{1,0:T(8,128)S(1)}, f32[128,128]{1,0:T(8,128)S(1)}, u32[]{:S(2)}, u32[]{:S(2)}) collective-permute-start(f32[128,128]{1,0:T(8,128)S(1)} %get-tuple-element.4.refs_0_), channel_id=1, source_target_pairs={{0,4},{1,5},{2,6},{3,7},{4,8},{5,9},{6,10},{7,11},{8,12},{9,13},{1... | collective-permute-start | bytes 196616 | tf_op jit(solution)/shard_map/ppermute | solution.py:348
  103.1 56.6 %copy-start = (s32[1,65536]{1,0:T(1,128)S(1)}, s32[1,65536]{1,0:T(1,128)}, u32[]{:S(2)}) copy-start(s32[1,65536]{1,0:T(1,128)} %param.12) | copy-start | bytes 786436
  130.0 4.6 %collective-permute-start.15 = (f32[16,128]{1,0:T(8,128)S(1)}, f32[16,128]{1,0:T(8,128)S(1)}, u32[]{:S(2)}, u32[]{:S(2)}) collective-permute-start(f32[16,128]{1,0:T(8,128)S(1)} %get-tuple-element.6), channel_id=1, source_target_pairs={{0,1},{1,2},{2,3},{3,0},{4,5},{5,6},{6,7},{7,4},{8,9},{9,10},{10,1... | collective-permute-start | bytes 24584 | tf_op jit(solution)/shard_map/ppermute | solution.py:367
  130.1 5.2 %collective-permute-start.14 = (f32[16,128]{1,0:T(8,128)S(1)}, f32[16,128]{1,0:T(8,128)S(1)}, u32[]{:S(2)}, u32[]{:S(2)}) collective-permute-start(f32[16,128]{1,0:T(8,128)S(1)} %get-tuple-element.7), channel_id=1, source_target_pairs={{0,2},{1,3},{2,0},{3,1},{4,6},{5,7},{6,4},{7,5},{8,10},{9,11},{10,... | collective-permute-start | bytes 24584 | tf_op jit(solution)/shard_map/ppermute | solution.py:367
  132.1 3.9 %collective-permute-start.13 = (f32[16,128]{1,0:T(8,128)S(1)}, f32[16,128]{1,0:T(8,128)S(1)}, u32[]{:S(2)}, u32[]{:S(2)}) collective-permute-start(f32[16,128]{1,0:T(8,128)S(1)} %get-tuple-element.8), channel_id=1, source_target_pairs={{0,3},{1,0},{2,1},{3,2},{4,7},{5,4},{6,5},{7,6},{8,11},{9,8},{10,9... | collective-permute-start | bytes 24584 | tf_op jit(solution)/shard_map/ppermute | solution.py:367
  136.0 10.0 %collective-permute-start.22 = (f32[16,128]{1,0:T(8,128)S(1)}, f32[16,128]{1,0:T(8,128)S(1)}, u32[]{:S(2)}, u32[]{:S(2)}) collective-permute-start(f32[16,128]{1,0:T(8,128)S(1)} %col_merge.1.refs_0_), channel_id=1, source_target_pairs={{0,224},{32,0},{64,32},{96,64},{128,96},{160,128},{192,160},{224,1... | collective-permute-start | bytes 24584 | tf_op jit(solution)/shard_map/ppermute | solution.py:370
  136.1 10.9 %collective-permute-start.21 = (f32[16,128]{1,0:T(8,128)S(1)}, f32[16,128]{1,0:T(8,128)S(1)}, u32[]{:S(2)}, u32[]{:S(2)}) collective-permute-start(f32[16,128]{1,0:T(8,128)S(1)} %col_merge.1.refs_0_), channel_id=1, source_target_pairs={{0,192},{32,224},{64,0},{96,32},{128,64},{160,96},{192,128},{224,1... | collective-permute-start | bytes 24584 | tf_op jit(solution)/shard_map/ppermute | solution.py:370
  138.4 10.7 %collective-permute-start.20 = (f32[16,128]{1,0:T(8,128)S(1)}, f32[16,128]{1,0:T(8,128)S(1)}, u32[]{:S(2)}, u32[]{:S(2)}) collective-permute-start(f32[16,128]{1,0:T(8,128)S(1)} %col_merge.1.refs_0_), channel_id=1, source_target_pairs={{0,160},{32,192},{64,224},{96,0},{128,32},{160,64},{192,96},{224,1... | collective-permute-start | bytes 24584 | tf_op jit(solution)/shard_map/ppermute | solution.py:370
  145.0 6.7 %collective-permute-start.19 = (f32[16,128]{1,0:T(8,128)S(1)}, f32[16,128]{1,0:T(8,128)S(1)}, u32[]{:S(2)}, u32[]{:S(2)}) collective-permute-start(f32[16,128]{1,0:T(8,128)S(1)} %col_merge.1.refs_0_), channel_id=1, source_target_pairs={{0,128},{32,160},{64,192},{96,224},{128,0},{160,32},{192,64},{224,... | collective-permute-start | bytes 24584 | tf_op jit(solution)/shard_map/ppermute | solution.py:370
  145.2 9.1 %collective-permute-start.18 = (f32[16,128]{1,0:T(8,128)S(1)}, f32[16,128]{1,0:T(8,128)S(1)}, u32[]{:S(2)}, u32[]{:S(2)}) collective-permute-start(f32[16,128]{1,0:T(8,128)S(1)} %col_merge.1.refs_0_), channel_id=1, source_target_pairs={{0,96},{32,128},{64,160},{96,192},{128,224},{160,0},{192,32},{224,... | collective-permute-start | bytes 24584 | tf_op jit(solution)/shard_map/ppermute | solution.py:370
  146.1 13.5 %collective-permute-start.12 = (f32[128,128]{1,0:T(8,128)S(1)}, f32[128,128]{1,0:T(8,128)S(1)}, u32[]{:S(2)}, u32[]{:S(2)}) collective-permute-start(f32[128,128]{1,0:T(8,128)S(1)} %row_merge.1.l0.lse), channel_id=1, source_target_pairs={{0,3},{1,0},{2,1},{3,2},{4,7},{5,4},{6,5},{7,6},{8,11},{9,8},{10,9... | collective-permute-start | bytes 196616 | tf_op jit(solution)/shard_map/ppermute | solution.py:350
  147.0 12.6 %collective-permute-start.11 = (f32[128,128]{1,0:T(8,128)S(1)}, f32[128,128]{1,0:T(8,128)S(1)}, u32[]{:S(2)}, u32[]{:S(2)}) collective-permute-start(f32[128,128]{1,0:T(8,128)S(1)} %row_merge.1.l0.lse), channel_id=1, source_target_pairs={{0,2},{1,3},{2,0},{3,1},{4,6},{5,7},{6,4},{7,5},{8,10},{9,11},{10,... | collective-permute-start | bytes 196616 | tf_op jit(solution)/shard_map/ppermute | solution.py:350
  149.1 10.5 %collective-permute-start.10 = (f32[128,128]{1,0:T(8,128)S(1)}, f32[128,128]{1,0:T(8,128)S(1)}, u32[]{:S(2)}, u32[]{:S(2)}) collective-permute-start(f32[128,128]{1,0:T(8,128)S(1)} %row_merge.1.l0.lse), channel_id=1, source_target_pairs={{0,1},{1,2},{2,3},{3,0},{4,5},{5,6},{6,7},{7,4},{8,9},{9,10},{10,1... | collective-permute-start | bytes 196616 | tf_op jit(solution)/shard_map/ppermute | solution.py:350
  151.7 4.9 %collective-permute-start.17 = (f32[16,128]{1,0:T(8,128)S(1)}, f32[16,128]{1,0:T(8,128)S(1)}, u32[]{:S(2)}, u32[]{:S(2)}) collective-permute-start(f32[16,128]{1,0:T(8,128)S(1)} %col_merge.1.refs_0_), channel_id=1, source_target_pairs={{0,64},{32,96},{64,128},{96,160},{128,192},{160,224},{192,0},{224,... | collective-permute-start | bytes 24584 | tf_op jit(solution)/shard_map/ppermute | solution.py:370
  154.3 4.3 %collective-permute-start.16 = (f32[16,128]{1,0:T(8,128)S(1)}, f32[16,128]{1,0:T(8,128)S(1)}, u32[]{:S(2)}, u32[]{:S(2)}) collective-permute-start(f32[16,128]{1,0:T(8,128)S(1)} %col_merge.1.refs_0_), channel_id=1, source_target_pairs={{0,32},{32,64},{64,96},{96,128},{128,160},{160,192},{192,224},{224... | collective-permute-start | bytes 24584 | tf_op jit(solution)/shard_map/ppermute | solution.py:370
  (9 other events, 226.9 us)

commit v2 on v1

v2 whole, which is shorter than its diff:
```python
import functools
import math

import jax
import jax.numpy as jnp
from jax import lax
from jax.experimental import pallas as pl
from jax.experimental.pallas import tpu as pltpu
from jax.sharding import PartitionSpec as P

PC = 32
BLK = 256
Z = 8
Y = 4
ROWS = 8
SRC = 65536
TGT = 2048
CHUNK = SRC // Y
NB = CHUNK // BLK
TB = TGT // BLK
CAP = 256
UNROLL = 8
SCATTER = 8
BUILD = 32
LOADS = 4
STORES = 4
PACK = 40
LOG2E = math.log2(math.e)
KAPPA = 10.0 * LOG2E
LN2 = math.log(2.0)
LOW = -1e30

f32 = jnp.float32
bf16 = jnp.bfloat16
NT = (((1,), (1,)), ((), ()))


def iota(shape, axis):
    return lax.broadcasted_iota(jnp.int32, shape, axis)


def indicator(condition):
    return jnp.where(condition, 1.0, 0.0).astype(bf16)


def three(value):
    first = value.astype(bf16).astype(f32)
    rest = value - first
    second = rest.astype(bf16).astype(f32)
    return first, second, rest - second


def vmem():
    return pl.BlockSpec(memory_space=pltpu.VMEM)


def anywhere():
    return pl.BlockSpec(memory_space=pl.ANY)


def smem():
    return pl.BlockSpec(memory_space=pltpu.SMEM)


def call(kernel, name, out_shape, in_specs, scratch, flops=0, nbytes=0, exps=0, limit=48, out_specs=None):
    many = isinstance(out_shape, (list, tuple))
    return pl.pallas_call(
        kernel,
        out_shape=out_shape,
        in_specs=in_specs,
        out_specs=out_specs or ([vmem() for _ in out_shape] if many else vmem()),
        scratch_shapes=scratch,
        compiler_params=pltpu.CompilerParams(vmem_limit_bytes=limit * 2**20),
        cost_estimate=pl.CostEstimate(flops=flops, bytes_accessed=nbytes, transcendentals=exps),
        name=name,
    )


def target_kernel(*refs):
    given, count, out, left, held, sems = refs[:5], refs[5], refs[6], refs[7], refs[8:13], refs[13]
    loads = [pltpu.make_async_copy(here, there, sems.at[k]) for k, (here, there) in enumerate(zip(given, held))]
    for load in loads:
        load.start()
    for load in loads:
        load.wait()
    coords, order, potential, which_source, which_target = held
    sub8 = iota((8, TGT), 0)
    vh, vm, vl = three(jnp.broadcast_to(potential[...], (8, TGT)))
    part = jnp.where(sub8 == 0, vh, jnp.where(sub8 == 1, vm, jnp.where(sub8 == 2, vl, 0.0)))
    left[0:32, :] = coords[...]
    left[32:48, :] = jnp.concatenate([part, jnp.zeros((8, TGT), f32)], axis=0).astype(bf16)
    number = iota((TGT, BLK), 0)

    def one_block(b, carry):
        span = pl.ds(pl.multiple_of(b * BLK, BLK), BLK)
        picked = indicator(number == order[:, span])
        got = jnp.dot(left[...], picked, preferred_element_type=f32)
        y = got[0:32]
        v = got[32:33] + got[33:34] + got[34:35]
        a = (v - jnp.sum(y * y, axis=0, keepdims=True) * (1.0 / PC)) * KAPPA
        out[0:32, span] = y
        out[32:40, span] = jnp.broadcast_to(a, (8, BLK))
        return carry

    lax.fori_loop(0, TB, one_block, 0)

    src = which_source[...]
    used = iota((1, CAP), 1) < count[0, 0]
    quarter = jnp.where(used, src // NB, 7)
    member = jnp.where(iota((8, CAP), 0) == quarter, 1.0, 0.0)
    earlier = indicator(iota((CAP, CAP), 0) < iota((CAP, CAP), 1))
    before = jnp.dot(member.astype(bf16), earlier, preferred_element_type=f32)
    rank = jnp.sum(member * before, axis=0, keepdims=True).astype(jnp.int32)
    place = quarter * CAP + rank
    sub16 = iota((16, CAP), 0)
    code = jnp.where(
        sub16 == 0,
        ((src % NB) * 8).astype(f32),
        jnp.where(sub16 == 1, (which_target[...] + 1).astype(f32), 0.0),
    ).astype(bf16)
    chosen = indicator(iota((Y * CAP, CAP), 0) == place)
    listed = lax.dot_general(code, chosen, NT, preferred_element_type=f32)
    out[39:40, 0 : Y * CAP] = listed[0:1] + listed[1:2]
    out[39:40, Y * CAP :] = jnp.zeros((1, TGT - Y * CAP), f32)


def gather_kernel(coords_all, mass_all, order_all, out_all, table, rows, coords, mass, order, out, sems, in_sem, out_sem):
    start = pl.multiple_of(lax.rem(lax.axis_index("col"), Y) * CHUNK, CHUNK)
    share = SRC // LOADS
    weights = pltpu.make_async_copy(mass_all, mass, in_sem.at[0])
    listed = pltpu.make_async_copy(order_all.at[:, pl.ds(start, CHUNK)], order, in_sem.at[1])
    loads = [
        pltpu.make_async_copy(
            coords_all.at[:, k * share : (k + 1) * share], coords.at[:, k * share : (k + 1) * share], sems.at[k]
        )
        for k in range(LOADS)
    ]
    weights.start()
    for load in loads:
        load.start()
    listed.start()
    sub8 = iota((8, 128), 0)
    lane = lax.rem(sub8, 4)
    first = jnp.where(sub8 == 0, 1.0, 0.0)
    blank = jnp.zeros((16, 128), bf16)

    def build(b):
        span = pl.ds(pl.multiple_of(b * 128, 128), 128)
        x = coords[:, span]
        wide = x.astype(f32)
        norm = jnp.sum(wide * wide, axis=0, keepdims=True) * (-KAPPA / PC)
        weight = mass[pl.ds(b, 1), :] * LOG2E
        both = jnp.where(sub8 < 4, jnp.broadcast_to(norm, (8, 128)), jnp.broadcast_to(weight, (8, 128)))
        h, m, l = three(both)
        part = jnp.where(lane == 0, h, jnp.where(lane == 1, m, jnp.where(lane == 2, l, 1.0)))
        part = jnp.concatenate([part, first], axis=0).astype(bf16)
        table[span, :] = jnp.concatenate([x, x, x, part, blank], axis=0).T.astype(f32)

    weights.wait()
    for k in range(LOADS):
        loads[k].wait()

        def several(g, carry):
            for u in range(BUILD):
                build(k * (share // 128) + g * BUILD + u)
            return carry

        lax.fori_loop(0, share // 128 // BUILD, several, 0)

    listed.wait()

    def one_block(b, carry):
        base = b * BLK
        for i in range(BLK):
            rows[pl.ds(i, 1), :] = table[pl.ds(order[0, base + i], 1), :]
        out[pl.ds(pl.multiple_of(base, BLK), BLK), :] = rows[...].astype(bf16)
        return carry

    share = CHUNK // STORES
    stores = []
    for k in range(STORES):
        lax.fori_loop(k * (NB // STORES), (k + 1) * (NB // STORES), one_block, 0)
        here = slice(k * share, (k + 1) * share)
        stores.append(pltpu.make_async_copy(out.at[here, :], out_all.at[here, :], out_sem.at[k]))
        stores[-1].start()
    for store in stores:
        store.wait()


def tiles(left_of, right_of, slot_of, highest, total, counts, codes, entries):
    filled = 0
    for d in range(Y):

        def copy(e, base):
            code = codes[d, e]
            entries[base + e] = code + (code // 8) * (TB * (Y - 1)) + d * TB
            return base

        lax.fori_loop(0, counts[d], copy, filled)
        filled = filled + counts[d]

    def tile(e):
        code = entries[e]
        s, t = code // (Y * TB), lax.rem(code, Y * TB)
        left = left_of(s, t)
        found = []
        for half in range(2):
            score = lax.dot_general(left, right_of(s, t, half), NT, preferred_element_type=f32)
            top = jnp.max(score, axis=0, keepdims=True)
            found.append((top, jnp.sum(jnp.exp2(score - top), axis=0, keepdims=True)))
        return slot_of(s, t), found

    def add(slot, found, has):
        for half, (top, summed) in enumerate(found):
            here = pl.ds(2 * slot + half, 1)
            top = jnp.where(has, top, LOW)
            old = highest[here, :]
            new = jnp.maximum(old, top)
            summed = jnp.where(has, summed, 0.0)
            total[here, :] = total[here, :] * jnp.exp2(old - new) + summed * jnp.exp2(top - new)
            highest[here, :] = new

    highest[...] = jnp.full(highest.shape, LOW, f32)
    total[...] = jnp.zeros(total.shape, f32)

    def several(g, carry):
        found = [tile(jnp.minimum(g * UNROLL + u, filled - 1)) for u in range(UNROLL)]
        for u in range(UNROLL):
            add(*found[u], g * UNROLL + u < filled)
        return carry

    lax.fori_loop(0, (filled + UNROLL - 1) // UNROLL, several, 0)
    return jnp.where(total[...] > 0.0, highest[...] + jnp.log2(total[...]), LOW)


def row_kernel(
    source_all, p0, p1, p2, p3, codes, counts, partial, late_all, source, late, early, highest, total, entries, sem
):
    load = pltpu.make_async_copy(source_all, source, sem.at[0])
    load.start()
    lane = iota((128, 128), 1)
    turned = indicator(((lane >= 100) & (lane <= 102)) | ((lane >= 105) & (lane <= 107)))
    sub8 = iota((8, 128), 0)
    for d, pack in enumerate((p0, p1, p2, p3)):

        def build(b, carry):
            span = pl.ds(pl.multiple_of(b * 128, 128), 128)
            h, m, l = three(pack[0:32, span] * (KAPPA / 16.0))
            ah, am, al = three(jnp.broadcast_to(pack[32:33, span], (8, 128)))
            part = jnp.where(sub8 < 3, 1.0, jnp.where(sub8 == 3, ah, jnp.where(sub8 == 7, am, 0.0)))
            last = jnp.where(sub8 == 0, al, 0.0)
            rows = jnp.concatenate([h, m, l, part, last, jnp.zeros((16, 128), f32)], axis=0).astype(bf16).T
            place = pl.ds(pl.multiple_of(d * TGT + b * 128, 128), 128)
            early[place, :] = rows
            late[place, :] = rows + turned
            return carry

        lax.fori_loop(0, TGT // 128, build, 0)

    store = pltpu.make_async_copy(late, late_all, sem.at[1])
    store.start()
    load.wait()
    partial[...] = tiles(
        lambda s, t: early[pl.ds(pl.multiple_of(t * BLK, BLK), BLK), :],
        lambda s, t, half: source[pl.ds(pl.multiple_of(s * BLK + half * 128, 128), 128), :],
        lambda s, t: s,
        highest,
        total,
        counts,
        codes,
        entries,
    )
    store.wait()


def merged(parts):
    top = functools.reduce(jnp.maximum, parts)
    return top + jnp.log2(sum(jnp.exp2(part - top) for part in parts))


def merge_kernel(*refs):
    refs[-1][...] = merged([ref[...] for ref in refs[:-1]])


def col_kernel(source_all, late_all, lse, codes, counts, partial, filled, late, highest, total, entries, sems):
    share = CHUNK // LOADS
    second = pltpu.make_async_copy(late_all, late, sems.at[LOADS])
    loads = []
    for k in range(LOADS):
        here = slice(k * share, (k + 1) * share)
        loads.append(pltpu.make_async_copy(source_all.at[here, :], filled.at[here, :], sems.at[k]))
        loads[-1].start()
    second.start()
    sub8 = iota((8, 128), 0)

    def fill(g, carry):
        for u in range(4):
            row = -lse[pl.ds(g * 4 + u, 1), :]
            h, m, l = three(jnp.broadcast_to(row, (8, 128)))
            part = jnp.where(sub8 == 1, h, jnp.where(sub8 == 2, m, jnp.where(sub8 == 3, l, 0.0)))
            rows = jnp.concatenate([jnp.zeros((104, 128), f32), part, jnp.zeros((16, 128), f32)], axis=0)
            span = pl.ds(pl.multiple_of((g * 4 + u) * 128, 128), 128)
            filled[span, :] = filled[span, :] + rows.astype(bf16).T
        return carry

    for k in range(LOADS):
        loads[k].wait()
        lax.fori_loop(k * (share // 512), (k + 1) * (share // 512), fill, 0)
    second.wait()
    partial[...] = tiles(
        lambda s, t: filled[pl.ds(pl.multiple_of(s * BLK, BLK), BLK), :],
        lambda s, t, half: late[pl.ds(pl.multiple_of(t * BLK + half * 128, 128), 128), :],
        lambda s, t: t,
        highest,
        total,
        counts,
        codes,
        entries,
    )


def flat(block):
    return jnp.concatenate([block[u : u + 1, :] for u in range(8)], axis=1)


def spread(order_row, value_row, high_rows):
    n = order_row.shape[1]
    high = indicator(iota((high_rows, n), 0) == order_row // 128)
    match = iota((128, n), 0) == lax.rem(order_row, 128)
    first = value_row.astype(bf16).astype(f32)
    low = jnp.concatenate(
        [jnp.where(match, first, 0.0), jnp.where(match, value_row - first, 0.0)], axis=0
    ).astype(bf16)
    return lax.dot_general(high, low, NT, preferred_element_type=f32)


def scatter_kernel(is_first, mass, order, lse, chunk, *refs):
    out, total = refs[-2:]
    number = iota((256, 1024), 0).astype(f32).astype(bf16)
    one, zero = jnp.ones((), bf16), jnp.zeros((), bf16)
    first = chunk[0] * (2 * NB)
    if is_first:
        total[...] = jnp.zeros(total.shape, f32)
    else:
        total[...] = refs[0][...]

    def product(g):
        cell = flat(order[pl.ds(pl.multiple_of(first + g * 8, 8), 8), :])
        value = flat(lse[pl.ds(pl.multiple_of(g * 8, 8), 8), :])
        column = lax.rem(cell // 128, 256).astype(f32).astype(bf16)
        row = (cell // 32768 * 128 + lax.rem(cell, 128)).astype(f32).astype(bf16)
        big = value.astype(bf16)
        small = (value - big.astype(f32)).astype(bf16)
        match = number == row
        left = jnp.concatenate([jnp.where(match, big, zero), jnp.where(match, small, zero)], axis=0)
        right = jnp.where(number == column, one, zero)
        return lax.dot_general(left, right, NT, preferred_element_type=f32)

    def step(g, carry):
        total[...] += sum(product(g * SCATTER + u) for u in range(SCATTER))
        return carry

    lax.fori_loop(0, NB // 4 // SCATTER, step, 0)
    if mass is None:
        out[...] = total[...]
        return
    for half in range(2):
        for side in range(2):
            here, rows = slice(side * 128, side * 128 + 128), half * 128
            both = total[rows : rows + 128, here] + total[256 + rows : 384 + rows, here]
            here = slice(half * 256 + side * 128, half * 256 + side * 128 + 128)
            out[here, :] = 0.1 * mass[here, :] - (0.1 * LN2) * both.T


def last_scatter_kernel(mass, *refs):
    scatter_kernel(False, mass, *refs)


def final_kernel(*refs):
    order, mass, potential, out = refs[4:]
    lse = merged([ref[...] for ref in refs[:4]])
    total = jnp.zeros((TGT // 128, 256), f32)
    for g in range(TGT // 1024):
        total += spread(flat(order[g * 8 : g * 8 + 8, :]), flat(lse[g * 8 : g * 8 + 8, :]), TGT // 128)
    out[...] = 0.1 * mass[...] + potential[...] - (0.1 * LN2) * (total[:, 0:128] + total[:, 128:256])


def y_shift(d):
    return [(z * Y + y, z * Y + (y + d) % Y) for z in range(Z) for y in range(Y)]


def z_shift(d):
    return [(z * Y + y, (z + d) % Z * Y + y) for z in range(Z) for y in range(Y)]


def z_pair():
    return [(z * Y + y, (z ^ 1) * Y + y) for z in range(Z) for y in range(Y)]


def row_pair():
    return [(r, r ^ 1) for r in range(ROWS)]


def row_shift(d):
    return [(r, (r + d) % ROWS) for r in range(ROWS)]


def body(
    source_coords,
    target_coords,
    source_order,
    target_order,
    source_mass,
    target_mass,
    target_potential,
    tile_source,
    tile_target,
    tile_count,
):
    shape = jax.ShapeDtypeStruct
    y = lax.rem(lax.axis_index("col"), Y)
    mass = source_mass.reshape(SRC // 128, 128)

    pack = call(
        target_kernel,
        "target_gather",
        shape((PACK, TGT), f32),
        [anywhere()] * 5 + [smem()],
        [
            pltpu.VMEM((48, TGT), bf16),
            pltpu.VMEM((PC, TGT), bf16),
            pltpu.VMEM((1, TGT), jnp.int32),
            pltpu.VMEM((1, TGT), f32),
            pltpu.VMEM((1, CAP), jnp.int32),
            pltpu.VMEM((1, CAP), jnp.int32),
            pltpu.SemaphoreType.DMA((5,)),
        ],
        flops=2 * 48 * TGT * TGT,
        limit=60,
    )(
        target_coords,
        target_order,
        target_potential.reshape(1, TGT),
        tile_source.reshape(1, CAP),
        tile_target.reshape(1, CAP),
        tile_count,
    )
    packs = [pack] + [lax.ppermute(pack, "col", y_shift(d)) for d in range(1, Y)]

    source = call(
        gather_kernel,
        "source_gather",
        shape((CHUNK, 128), bf16),
        [anywhere()] * 3,
        [
            pltpu.VMEM((SRC, 128), f32),
            pltpu.VMEM((BLK, 128), f32),
            pltpu.VMEM((PC, SRC), bf16),
            pltpu.VMEM((SRC // 128, 128), f32),
            pltpu.SMEM((1, CHUNK), jnp.int32),
            pltpu.VMEM((CHUNK, 128), bf16),
            pltpu.SemaphoreType.DMA((LOADS,)),
            pltpu.SemaphoreType.DMA((2,)),
            pltpu.SemaphoreType.DMA((STORES,)),
        ],
        flops=2 * 10**10,
        nbytes=64 * 2**20,
        limit=56,
        out_specs=anywhere(),
    )(source_coords, mass, source_order)

    lists = jnp.concatenate([lax.dynamic_slice(p, (PACK - 1, y * CAP), (1, CAP)) for p in packs], axis=0)
    codes = lists.astype(jnp.int32) - 1
    counts = jnp.sum((lists > 0.5).astype(jnp.int32), axis=1)

    partial, late = call(
        row_kernel,
        "row_pass",
        [shape((2 * NB, 128), f32), shape((Y * TGT, 128), bf16)],
        [anywhere()] + [vmem()] * 4 + [smem()] * 2,
        [
            pltpu.VMEM((CHUNK, 128), bf16),
            pltpu.VMEM((Y * TGT, 128), bf16),
            pltpu.VMEM((Y * TGT, 128), bf16),
            pltpu.VMEM((2 * NB, 128), f32),
            pltpu.VMEM((2 * NB, 128), f32),
            pltpu.SMEM((Y * CAP,), jnp.int32),
            pltpu.SemaphoreType.DMA((2,)),
        ],
        out_specs=[vmem(), anywhere()],
    )(source, *packs, codes, counts)

    partials = [partial] + [lax.ppermute(partial, "col", z_shift(d)) for d in (2, 4, 6)]
    lse = call(merge_kernel, "row_merge_four", shape((2 * NB, 128), f32), [vmem()] * 4, [])(*partials)
    partials = [lse, lax.ppermute(lse, "col", z_pair())]
    lse = call(merge_kernel, "row_merge_two", shape((2 * NB, 128), f32), [vmem()] * 2, [])(*partials)
    lses = [lse] + [lax.ppermute(lse, "col", y_shift(d)) for d in range(1, Y)]

    target_partial = call(
        col_kernel,
        "col_pass",
        shape((2 * Y * TB, 128), f32),
        [anywhere(), anywhere(), vmem()] + [smem()] * 2,
        [
            pltpu.VMEM((CHUNK, 128), bf16),
            pltpu.VMEM((Y * TGT, 128), bf16),
            pltpu.VMEM((2 * Y * TB, 128), f32),
            pltpu.VMEM((2 * Y * TB, 128), f32),
            pltpu.SMEM((Y * CAP,), jnp.int32),
            pltpu.SemaphoreType.DMA((LOADS + 1,)),
        ],
        flops=2 * 10**10,
        exps=10**7,
    )(source, late, lse, codes, counts)

    order_rows = source_order.reshape(SRC // 128, 128)
    cost = dict(flops=2 * 512 * 256 * CHUNK, nbytes=2**20)
    totals = shape((512, 256), f32)
    keep = [pltpu.VMEM((512, 256), f32)]

    def piece(d, before=None):
        chunk = lax.rem(y + Y - d, Y).reshape(1)
        kernel = functools.partial(scatter_kernel, before is None, None)
        return call(
            kernel, f"source_scatter_{d}", totals, [vmem()] * 2 + [smem()] + [vmem()] * (before is not None), keep, **cost
        )(order_rows, lses[d], chunk, *([] if before is None else [before]))

    own = [target_partial[0 : 2 * TB]] + [
        lax.ppermute(target_partial[2 * d * TB : 2 * (d + 1) * TB], "col", y_shift(-d)) for d in range(1, Y)
    ]
    scattered = piece(0)
    own, scattered = lax.optimization_barrier((own, scattered))
    merge = lambda name, parts: call(merge_kernel, name, shape((2 * TB, 128), f32), [vmem()] * len(parts), [])(*parts)
    own = merge("col_merge_y", own)
    own = [own, lax.ppermute(own, "row", row_pair())]
    scattered = piece(1, scattered)
    own, scattered = lax.optimization_barrier((own, scattered))
    own = merge("col_merge_core", own)
    own = [own] + [lax.ppermute(own, "row", row_shift(d)) for d in (2, 4, 6)]
    scattered = piece(2, scattered)
    source_update = call(
        last_scatter_kernel,
        "source_scatter_3",
        shape((SRC // 128, 128), f32),
        [vmem()] * 3 + [smem(), vmem()],
        keep,
        **cost,
    )(mass, order_rows, lses[3], lax.rem(y + Y - 3, Y).reshape(1), scattered)
    own, source_update = lax.optimization_barrier((own, source_update))
    target_update = call(
        final_kernel,
        "target_scatter",
        shape((TGT // 128, 128), f32),
        [vmem()] * 7,
        [],
    )(
        *own,
        target_order.reshape(TGT // 128, 128),
        target_mass.reshape(TGT // 128, 128),
        target_potential.reshape(TGT // 128, 128),
    )
    return (source_update.reshape(SRC), target_update.reshape(TGT))


def solution(mesh):
    in_specs = (
        P(None, "row"),
        P(None, "col"),
        P("row", None),
        P("col", None),
        P("row"),
        P("col"),
        P("col"),
        P("row", "col", None),
        P("row", "col", None),
        P("row", "col"),
    )
    out_specs = (P("row"), P("col"))
    return jax.shard_map(body, mesh=mesh, in_specs=in_specs, out_specs=out_specs, check_vma=False)
```

time: 194 us -> 122 us (0.63)
  the two profiles are of different devices: /device:TPU:40 before, /device:TPU:1 now
where the time goes in v2:
time: 122 us; the launch traced here: 124 us
  Pallas kernels  74.6 us (61%)
  starting transfers between devices  43.3 us (35%)
  waiting for transfers between devices  3.97 us (3%)
  between operations  1.47 us (1%)
    pallas_call x1, Pallas kernels, body(): call(gather_kernel, 'source_gather', shape((CHUNK, 128), bf16), [anywhere...  22.5 us
    pallas_call x3, Pallas kernels, piece(): call(kernel, f'source_scatter_{d}', totals, [vmem()] * 2 + [smem()] + [vm...  14.5 us
    pallas_call x1, Pallas kernels, body(): call(row_kernel, 'row_pass', [shape((2 * NB, 128), f32), shape((Y * TGT,...  13.4 us
    pallas_call x1, Pallas kernels, body(): call(col_kernel, 'col_pass', shape((2 * Y * TB, 128), f32), [anywhere(),...  12.8 us
    ppermute x3, starting transfers between devices, body(): lax.ppermute(partial, 'col', z_shift(d))  11.9 us
    ppermute x3, starting transfers between devices, body(): own = [own] + [lax.ppermute(own, 'row', row_shift(d)) for d in (2, 4, 6)]  8.14 us
    ppermute x1, starting transfers between devices, body(): own = [own, lax.ppermute(own, 'row', row_pair())]  8.05 us
    pallas_call x1, Pallas kernels, body(): call(last_scatter_kernel, 'source_scatter_3', shape((SRC // 128, 128), f3...  5.65 us
  transfers between devices with their start and end apart: 17, of which 2 were waited for; matrix products, arithmetic and copies ran while one was open for 0% of the time, Pallas kernels for 45%

profile of v2, /device:TPU:1, one launch (start us, length us, event | category | flops | bytes accessed | tf_op | source)
XLA Modules:
  0.0 123.8 jit_solution(4433369273261585641)
XLA Ops:
  1.3 4.6 %target_gather.1.p0 = f32[40,2048]{1,0:T(8,128)} custom-call(bf16[32,2048]{1,0:T(8,128)(2,1)} %refs_0_.1, s32[1,2048]{1,0:T(1,128)} %refs_1_.1, f32[1,2048]{1,0:T(1,128)} %bitcast.15, s32[1,256]{1,0:T(1,128)} %bitcast.25, s32[1,256]{1,0:T(1,128)} %bitcast.26, s32[1,1]{1,0:T(1,128)S(6)} %copy.12.refs_5_), custom_call_target="tpu_custom_call" | custom-call | flops 402653184 | tf_op jit(solution)/shard_map/target_gather/pallas_call | solution.py:424
  5.9 3.6 %collective-permute-start.2 = (f32[40,2048]{1,0:T(8,128)}, f32[40,2048]{1,0:T(8,128)S(1)}, u32[]{:S(2)}, u32[]{:S(2)}) collective-permute-start(f32[40,2048]{1,0:T(8,128)} %target_gather.1.p0), channel_id=1, source_target_pairs={{0,3},{1,0},{2,1},{3,2},{4,7},{5,4},{6,5},{7,6},{8,11},{9,8},{10,9... | collective-permute-start | bytes 983048 | tf_op jit(solution)/shard_map/ppermute | solution.py:448
  9.9 0.7 collective-permute-start
  10.6 22.5 %source_gather.1.source_all = bf16[16384,128]{1,0:T(8,128)(2,1)} custom-call(bf16[32,65536]{1,0:T(8,128)(2,1)} %coords_all.1, f32[512,128]{1,0:T(8,128)} %bitcast.18, s32[1,65536]{1,0:T(1,128)} %order_all.1), custom_call_target="tpu_custom_call" | custom-call | flops 20000000000 | bytes 67108864 | tf_op jit(solution)/shard_map/source_gather/pallas_call | solution.py:450
  33.6 13.4 %row_pass.1 = (f32[128,128]{1,0:T(8,128)S(1)}, bf16[8192,128]{1,0:T(8,128)(2,1)S(1)}) custom-call(bf16[16384,128]{1,0:T(8,128)(2,1)} %source_gather.1.source_all, f32[40,2048]{1,0:T(8,128)S(1)} %copy-done, f32[40,2048]{1,0:T(8,128)S(1)} %collective-permute-done.p1, f32[40,2048]{1,0:T(8,128)S(1)} %collective-permute-done.1.p2, ...), custom_call_target="tpu_custom_call" | custom-call | tf_op jit(solution)/shard_map/row_pass/pallas_call | solution.py:476
  46.9 4.5 %collective-permute-start.3 = (f32[128,128]{1,0:T(8,128)S(1)}, f32[128,128]{1,0:T(8,128)S(1)}, u32[]{:S(2)}, u32[]{:S(2)}) collective-permute-start(f32[128,128]{1,0:T(8,128)S(1)} %get-tuple-element.18.refs_0_), channel_id=1, source_target_pairs={{0,8},{1,9},{2,10},{3,11},{4,12},{5,13},{6,14},{7,15},{8,16},{9,17... | collective-permute-start | bytes 196616 | tf_op jit(solution)/shard_map/ppermute | solution.py:493
  51.4 4.0 %collective-permute-start.4 = (f32[128,128]{1,0:T(8,128)S(1)}, f32[128,128]{1,0:T(8,128)S(1)}, u32[]{:S(2)}, u32[]{:S(2)}) collective-permute-start(f32[128,128]{1,0:T(8,128)S(1)} %get-tuple-element.18.refs_0_), channel_id=1, source_target_pairs={{0,16},{1,17},{2,18},{3,19},{4,20},{5,21},{6,22},{7,23},{8,24},{9,... | collective-permute-start | bytes 196616 | tf_op jit(solution)/shard_map/ppermute | solution.py:493
  55.4 3.5 %collective-permute-start.5 = (f32[128,128]{1,0:T(8,128)S(1)}, f32[128,128]{1,0:T(8,128)S(1)}, u32[]{:S(2)}, u32[]{:S(2)}) collective-permute-start(f32[128,128]{1,0:T(8,128)S(1)} %get-tuple-element.18.refs_0_), channel_id=1, source_target_pairs={{0,24},{1,25},{2,26},{3,27},{4,28},{5,29},{6,30},{7,31},{8,0},{9,1... | collective-permute-start | bytes 196616 | tf_op jit(solution)/shard_map/ppermute | solution.py:493
  58.9 1.3 %collective-permute-done.5.refs_3_ = f32[128,128]{1,0:T(8,128)S(1)} collective-permute-done((f32[128,128]{1,0:T(8,128)S(1)}, f32[128,128]{1,0:T(8,128)S(1)}, u32[]{:S(2)}, u32[]{:S(2)}) %collective-permute-start.5) | collective-permute-done | bytes 65568 | tf_op jit(solution)/shard_map/ppermute | solution.py:493
  60.3 2.1 %collective-permute-start.6 = (f32[128,128]{1,0:T(8,128)S(1)}, f32[128,128]{1,0:T(8,128)S(1)}, u32[]{:S(2)}, u32[]{:S(2)}) collective-permute-start(f32[128,128]{1,0:T(8,128)S(1)} %row_merge_four.1.refs_0_), channel_id=1, source_target_pairs={{0,4},{1,5},{2,6},{3,7},{4,0},{5,1},{6,2},{7,3},{8,12},{9,13},{10,... | collective-permute-start | bytes 196616 | tf_op jit(solution)/shard_map/ppermute | solution.py:495
  62.4 2.6 %collective-permute-done.6.refs_1_ = f32[128,128]{1,0:T(8,128)S(1)} collective-permute-done((f32[128,128]{1,0:T(8,128)S(1)}, f32[128,128]{1,0:T(8,128)S(1)}, u32[]{:S(2)}, u32[]{:S(2)}) %collective-permute-start.6) | collective-permute-done | bytes 65568 | tf_op jit(solution)/shard_map/ppermute | solution.py:495
  65.0 2.3 %collective-permute-start.11 = (f32[128,128]{1,0:T(8,128)S(1)}, f32[128,128]{1,0:T(8,128)S(1)}, u32[]{:S(2)}, u32[]{:S(2)}) collective-permute-start(f32[128,128]{1,0:T(8,128)S(1)} %row_merge_two.1.lse), channel_id=1, source_target_pairs={{0,1},{1,2},{2,3},{3,0},{4,5},{5,6},{6,7},{7,4},{8,9},{9,10},{10,1... | collective-permute-start | bytes 196616 | tf_op jit(solution)/shard_map/ppermute | solution.py:497
  67.3 1.1 collective-permute-start.16
  68.3 12.8 %col_pass.1 = f32[64,128]{1,0:T(8,128)S(1)} custom-call(bf16[16384,128]{1,0:T(8,128)(2,1)} %source_gather.1.source_all, bf16[8192,128]{1,0:T(8,128)(2,1)S(1)} %get-tuple-element.17.late_all, f32[128,128]{1,0:T(8,128)S(1)} %row_merge_two.1.lse, s32[4,256]{1,0:T(4,128)S(1)} %get-tuple-element.37.codes, s32[4]{0:T(128)S(1)} %get-tuple-element.36.counts), custom_call_target="tpu_custom_call" | custom-call | flops 20000000000 | tf_op jit(solution)/shard_map/col_pass/pallas_call | solution.py:499
  81.8 1.7 %collective-permute-start.8 = (f32[16,128]{1,0:T(8,128)S(1)}, f32[16,128]{1,0:T(8,128)S(1)}, u32[]{:S(2)}, u32[]{:S(2)}) collective-permute-start(f32[16,128]{1,0:T(8,128)S(1)} %get-tuple-element.33), channel_id=1, source_target_pairs={{0,2},{1,3},{2,0},{3,1},{4,6},{5,7},{6,4},{7,5},{8,10},{9,11},{10,... | collective-permute-start | bytes 24584 | tf_op jit(solution)/shard_map/ppermute | solution.py:529
  84.0 4.8 %source_scatter_0.1.refs_0_ = f32[512,256]{1,0:T(8,128)S(1)} custom-call(s32[512,128]{1,0:T(8,128)S(1)} %bitcast.20, f32[128,128]{1,0:T(8,128)S(1)} %row_merge_two.1.lse, s32[1]{0:T(128)} %bitcast.5.chunk), custom_call_target="tpu_custom_call" | custom-call | flops 4294967296 | bytes 1048576 | tf_op jit(solution)/shard_map/source_scatter_0/pallas_call | solution.py:524
  88.9 2.2 %collective-permute-start.15 = (f32[128,128]{1,0:T(8,128)S(1)}, f32[128,128]{1,0:T(8,128)S(1)}, u32[]{:S(2)}, u32[]{:S(2)}) collective-permute-start(f32[128,128]{1,0:T(8,128)S(1)} %row_merge_two.1.lse), channel_id=1, source_target_pairs={{0,3},{1,0},{2,1},{3,2},{4,7},{5,4},{6,5},{7,6},{8,11},{9,8},{10,9... | collective-permute-start | bytes 196616 | tf_op jit(solution)/shard_map/ppermute | solution.py:497
  91.1 8.1 %collective-permute-start.10 = (f32[16,128]{1,0:T(8,128)S(1)}, f32[16,128]{1,0:T(8,128)S(1)}, u32[]{:S(2)}, u32[]{:S(2)}) collective-permute-start(f32[16,128]{1,0:T(8,128)S(1)} %col_merge_y.1.refs_0_), channel_id=1, source_target_pairs={{0,32},{32,0},{64,96},{96,64},{128,160},{160,128},{192,224},{224,1... | collective-permute-start | bytes 24584 | tf_op jit(solution)/shard_map/ppermute | solution.py:535
  99.1 4.8 %source_scatter_1.1.refs_0_ = f32[512,256]{1,0:T(8,128)S(1)} custom-call(s32[512,128]{1,0:T(8,128)S(1)} %bitcast.21, f32[128,128]{1,0:T(8,128)S(1)} %collective-permute-done.11.lse, s32[1]{0:T(128)} %bitcast.6.chunk, f32[512,256]{1,0:T(8,128)S(1)} %source_scatter_0.1.refs_0_), custom_call_target="tpu_custom_call" | custom-call | flops 4294967296 | bytes 1048576 | tf_op jit(solution)/shard_map/source_scatter_1/pallas_call | solution.py:524
  104.4 5.8 %collective-permute-start.13 = (f32[16,128]{1,0:T(8,128)S(1)}, f32[16,128]{1,0:T(8,128)S(1)}, u32[]{:S(2)}, u32[]{:S(2)}) collective-permute-start(f32[16,128]{1,0:T(8,128)S(1)} %col_merge_core.1.refs_0_), channel_id=1, source_target_pairs={{0,128},{32,160},{64,192},{96,224},{128,0},{160,32},{192,64},{224,... | collective-permute-start | bytes 24584 | tf_op jit(solution)/shard_map/ppermute | solution.py:539
  110.2 2.0 %collective-permute-start.14 = (f32[16,128]{1,0:T(8,128)S(1)}, f32[16,128]{1,0:T(8,128)S(1)}, u32[]{:S(2)}, u32[]{:S(2)}) collective-permute-start(f32[16,128]{1,0:T(8,128)S(1)} %col_merge_core.1.refs_0_), channel_id=1, source_target_pairs={{0,192},{32,224},{64,0},{96,32},{128,64},{160,96},{192,128},{224,1... | collective-permute-start | bytes 24584 | tf_op jit(solution)/shard_map/ppermute | solution.py:539
  112.2 4.8 %source_scatter_2.1.refs_3_ = f32[512,256]{1,0:T(8,128)S(1)} custom-call(s32[512,128]{1,0:T(8,128)S(1)} %bitcast.22, f32[128,128]{1,0:T(8,128)S(1)} %collective-permute-done.16.lse, s32[1]{0:T(128)} %bitcast.8.chunk, f32[512,256]{1,0:T(8,128)S(1)} %source_scatter_1.1.refs_0_), custom_call_target="tpu_custom_call" | custom-call | flops 4294967296 | bytes 1048576 | tf_op jit(solution)/shard_map/source_scatter_2/pallas_call | solution.py:524
  117.0 5.6 %source_scatter_3.1 = f32[512,128]{1,0:T(8,128)} custom-call(f32[512,128]{1,0:T(8,128)S(1)} %bitcast.19, s32[512,128]{1,0:T(8,128)S(1)} %bitcast.23, f32[128,128]{1,0:T(8,128)S(1)} %collective-permute-done.15.refs_1_, s32[1]{0:T(128)} %bitcast.7.refs_2_, f32[512,256]{1,0:T(8,128)S(1)} %source_scatter_2.1.refs_3_), custom_call_target="tpu_custom_call" | custom-call | flops 4294967296 | bytes 1048576 | tf_op jit(solution)/shard_map/source_scatter_3/pallas_call | solution.py:541
  122.7 1.0 target_scatter.1
  (41 shorter events, 2.6 us)
Async XLA Ops:
  5.9 27.3 %collective-permute-start.2 = (f32[40,2048]{1,0:T(8,128)}, f32[40,2048]{1,0:T(8,128)S(1)}, u32[]{:S(2)}, u32[]{:S(2)}) collective-permute-start(f32[40,2048]{1,0:T(8,128)} %target_gather.1.p0), channel_id=1, source_target_pairs={{0,3},{1,0},{2,1},{3,2},{4,7},{5,4},{6,5},{7,6},{8,11},{9,8},{10,9... | collective-permute-start | bytes 983048 | tf_op jit(solution)/shard_map/ppermute | solution.py:448
  9.5 23.8 %collective-permute-start.1 = (f32[40,2048]{1,0:T(8,128)}, f32[40,2048]{1,0:T(8,128)S(1)}, u32[]{:S(2)}, u32[]{:S(2)}) collective-permute-start(f32[40,2048]{1,0:T(8,128)} %target_gather.1.p0), channel_id=1, source_target_pairs={{0,2},{1,3},{2,0},{3,1},{4,6},{5,7},{6,4},{7,5},{8,10},{9,11},{10,... | collective-permute-start | bytes 983048 | tf_op jit(solution)/shard_map/ppermute | solution.py:448
  9.9 23.5 %collective-permute-start = (f32[40,2048]{1,0:T(8,128)}, f32[40,2048]{1,0:T(8,128)S(1)}, u32[]{:S(2)}, u32[]{:S(2)}) collective-permute-start(f32[40,2048]{1,0:T(8,128)} %target_gather.1.p0), channel_id=1, source_target_pairs={{0,1},{1,2},{2,3},{3,0},{4,5},{5,6},{6,7},{7,4},{8,9},{9,10},{10,1... | collective-permute-start | bytes 983048 | tf_op jit(solution)/shard_map/ppermute | solution.py:448
  10.6 22.5 %copy-start = (f32[40,2048]{1,0:T(8,128)S(1)}, f32[40,2048]{1,0:T(8,128)}, u32[]{:S(2)}) copy-start(f32[40,2048]{1,0:T(8,128)} %target_gather.1.p0) | copy-start | bytes 983044
  46.9 11.9 %collective-permute-start.3 = (f32[128,128]{1,0:T(8,128)S(1)}, f32[128,128]{1,0:T(8,128)S(1)}, u32[]{:S(2)}, u32[]{:S(2)}) collective-permute-start(f32[128,128]{1,0:T(8,128)S(1)} %get-tuple-element.18.refs_0_), channel_id=1, source_target_pairs={{0,8},{1,9},{2,10},{3,11},{4,12},{5,13},{6,14},{7,15},{8,16},{9,17... | collective-permute-start | bytes 196616 | tf_op jit(solution)/shard_map/ppermute | solution.py:493
  51.4 7.5 %collective-permute-start.4 = (f32[128,128]{1,0:T(8,128)S(1)}, f32[128,128]{1,0:T(8,128)S(1)}, u32[]{:S(2)}, u32[]{:S(2)}) collective-permute-start(f32[128,128]{1,0:T(8,128)S(1)} %get-tuple-element.18.refs_0_), channel_id=1, source_target_pairs={{0,16},{1,17},{2,18},{3,19},{4,20},{5,21},{6,22},{7,23},{8,24},{9,... | collective-permute-start | bytes 196616 | tf_op jit(solution)/shard_map/ppermute | solution.py:493
  55.4 4.8 %collective-permute-start.5 = (f32[128,128]{1,0:T(8,128)S(1)}, f32[128,128]{1,0:T(8,128)S(1)}, u32[]{:S(2)}, u32[]{:S(2)}) collective-permute-start(f32[128,128]{1,0:T(8,128)S(1)} %get-tuple-element.18.refs_0_), channel_id=1, source_target_pairs={{0,24},{1,25},{2,26},{3,27},{4,28},{5,29},{6,30},{7,31},{8,0},{9,1... | collective-permute-start | bytes 196616 | tf_op jit(solution)/shard_map/ppermute | solution.py:493
  60.3 4.7 %collective-permute-start.6 = (f32[128,128]{1,0:T(8,128)S(1)}, f32[128,128]{1,0:T(8,128)S(1)}, u32[]{:S(2)}, u32[]{:S(2)}) collective-permute-start(f32[128,128]{1,0:T(8,128)S(1)} %row_merge_four.1.refs_0_), channel_id=1, source_target_pairs={{0,4},{1,5},{2,6},{3,7},{4,0},{5,1},{6,2},{7,3},{8,12},{9,13},{10,... | collective-permute-start | bytes 196616 | tf_op jit(solution)/shard_map/ppermute | solution.py:495
  65.0 34.1 %collective-permute-start.11 = (f32[128,128]{1,0:T(8,128)S(1)}, f32[128,128]{1,0:T(8,128)S(1)}, u32[]{:S(2)}, u32[]{:S(2)}) collective-permute-start(f32[128,128]{1,0:T(8,128)S(1)} %row_merge_two.1.lse), channel_id=1, source_target_pairs={{0,1},{1,2},{2,3},{3,0},{4,5},{5,6},{6,7},{7,4},{8,9},{9,10},{10,1... | collective-permute-start | bytes 196616 | tf_op jit(solution)/shard_map/ppermute | solution.py:497
  67.3 44.9 %collective-permute-start.16 = (f32[128,128]{1,0:T(8,128)S(1)}, f32[128,128]{1,0:T(8,128)S(1)}, u32[]{:S(2)}, u32[]{:S(2)}) collective-permute-start(f32[128,128]{1,0:T(8,128)S(1)} %row_merge_two.1.lse), channel_id=1, source_target_pairs={{0,2},{1,3},{2,0},{3,1},{4,6},{5,7},{6,4},{7,5},{8,10},{9,11},{10,... | collective-permute-start | bytes 196616 | tf_op jit(solution)/shard_map/ppermute | solution.py:497
  68.3 15.7 %copy-start.5 = (s32[1,65536]{1,0:T(1,128)S(1)}, s32[1,65536]{1,0:T(1,128)}, u32[]{:S(2)}) copy-start(s32[1,65536]{1,0:T(1,128)} %order_all.1) | copy-start | bytes 786436
  81.2 7.7 %collective-permute-start.7 = (f32[16,128]{1,0:T(8,128)S(1)}, f32[16,128]{1,0:T(8,128)S(1)}, u32[]{:S(2)}, u32[]{:S(2)}) collective-permute-start(f32[16,128]{1,0:T(8,128)S(1)} %get-tuple-element.34), channel_id=1, source_target_pairs={{0,3},{1,0},{2,1},{3,2},{4,7},{5,4},{6,5},{7,6},{8,11},{9,8},{10,9... | collective-permute-start | bytes 24584 | tf_op jit(solution)/shard_map/ppermute | solution.py:529
  81.8 9.3 %collective-permute-start.8 = (f32[16,128]{1,0:T(8,128)S(1)}, f32[16,128]{1,0:T(8,128)S(1)}, u32[]{:S(2)}, u32[]{:S(2)}) collective-permute-start(f32[16,128]{1,0:T(8,128)S(1)} %get-tuple-element.33), channel_id=1, source_target_pairs={{0,2},{1,3},{2,0},{3,1},{4,6},{5,7},{6,4},{7,5},{8,10},{9,11},{10,... | collective-permute-start | bytes 24584 | tf_op jit(solution)/shard_map/ppermute | solution.py:529
  83.5 7.6 %collective-permute-start.9 = (f32[16,128]{1,0:T(8,128)S(1)}, f32[16,128]{1,0:T(8,128)S(1)}, u32[]{:S(2)}, u32[]{:S(2)}) collective-permute-start(f32[16,128]{1,0:T(8,128)S(1)} %get-tuple-element.32), channel_id=1, source_target_pairs={{0,1},{1,2},{2,3},{3,0},{4,5},{5,6},{6,7},{7,4},{8,9},{9,10},{10,1... | collective-permute-start | bytes 24584 | tf_op jit(solution)/shard_map/ppermute | solution.py:529
  88.9 28.1 %collective-permute-start.15 = (f32[128,128]{1,0:T(8,128)S(1)}, f32[128,128]{1,0:T(8,128)S(1)}, u32[]{:S(2)}, u32[]{:S(2)}) collective-permute-start(f32[128,128]{1,0:T(8,128)S(1)} %row_merge_two.1.lse), channel_id=1, source_target_pairs={{0,3},{1,0},{2,1},{3,2},{4,7},{5,4},{6,5},{7,6},{8,11},{9,8},{10,9... | collective-permute-start | bytes 196616 | tf_op jit(solution)/shard_map/ppermute | solution.py:497
  91.1 12.9 %collective-permute-start.10 = (f32[16,128]{1,0:T(8,128)S(1)}, f32[16,128]{1,0:T(8,128)S(1)}, u32[]{:S(2)}, u32[]{:S(2)}) collective-permute-start(f32[16,128]{1,0:T(8,128)S(1)} %col_merge_y.1.refs_0_), channel_id=1, source_target_pairs={{0,32},{32,0},{64,96},{96,64},{128,160},{160,128},{192,224},{224,1... | collective-permute-start | bytes 24584 | tf_op jit(solution)/shard_map/ppermute | solution.py:535
  104.0 18.7 %collective-permute-start.12 = (f32[16,128]{1,0:T(8,128)S(1)}, f32[16,128]{1,0:T(8,128)S(1)}, u32[]{:S(2)}, u32[]{:S(2)}) collective-permute-start(f32[16,128]{1,0:T(8,128)S(1)} %col_merge_core.1.refs_0_), channel_id=1, source_target_pairs={{0,64},{32,96},{64,128},{96,160},{128,192},{160,224},{192,0},{224,... | collective-permute-start | bytes 24584 | tf_op jit(solution)/shard_map/ppermute | solution.py:539
  104.4 18.3 %collective-permute-start.13 = (f32[16,128]{1,0:T(8,128)S(1)}, f32[16,128]{1,0:T(8,128)S(1)}, u32[]{:S(2)}, u32[]{:S(2)}) collective-permute-start(f32[16,128]{1,0:T(8,128)S(1)} %col_merge_core.1.refs_0_), channel_id=1, source_target_pairs={{0,128},{32,160},{64,192},{96,224},{128,0},{160,32},{192,64},{224,... | collective-permute-start | bytes 24584 | tf_op jit(solution)/shard_map/ppermute | solution.py:539
  110.2 12.5 %collective-permute-start.14 = (f32[16,128]{1,0:T(8,128)S(1)}, f32[16,128]{1,0:T(8,128)S(1)}, u32[]{:S(2)}, u32[]{:S(2)}) collective-permute-start(f32[16,128]{1,0:T(8,128)S(1)} %col_merge_core.1.refs_0_), channel_id=1, source_target_pairs={{0,192},{32,224},{64,0},{96,32},{128,64},{160,96},{192,128},{224,1... | collective-permute-start | bytes 24584 | tf_op jit(solution)/shard_map/ppermute | solution.py:539
  112.2 4.8 %copy-start.4 = (f32[65536]{0:T(1024)S(1)}, f32[65536]{0:T(1024)}, u32[]{:S(2)}) copy-start(f32[65536]{0:T(1024)} %param.14) | copy-start | bytes 786436
  117.0 5.7 %copy-start.1 = (s32[1,2048]{1,0:T(1,128)S(1)}, s32[1,2048]{1,0:T(1,128)}, u32[]{:S(2)}) copy-start(s32[1,2048]{1,0:T(1,128)} %refs_1_.1) | copy-start | bytes 24580
  117.0 5.7 %copy-start.2 = (f32[2048]{0:T(1024)S(1)}, f32[2048]{0:T(1024)}, u32[]{:S(2)}) copy-start(f32[2048]{0:T(1024)} %param.16) | copy-start | bytes 24580
  117.0 5.7 %copy-start.3 = (f32[2048]{0:T(1024)S(1)}, f32[2048]{0:T(1024)}, u32[]{:S(2)}) copy-start(f32[2048]{0:T(1024)} %param.15) | copy-start | bytes 24580

commit v3 on v2

--- a/solution.py
+++ b/solution.py
@@ -19,7 +19,7 @@
 NB = CHUNK // BLK
 TB = TGT // BLK
 CAP = 256
-UNROLL = 8
+UNROLL = 16
 SCATTER = 8
 BUILD = 32
 LOADS = 4
@@ -334,50 +334,55 @@
     return lax.dot_general(high, low, NT, preferred_element_type=f32)
 
 
-def scatter_kernel(is_first, mass, order, lse, chunk, *refs):
+def scatter_kernel(mass, order, first_lse, second_lse, chunk, *refs):
+    half = lax.rem(lax.axis_index("col") // Y, 2)
     out, total = refs[-2:]
     number = iota((256, 1024), 0).astype(f32).astype(bf16)
     one, zero = jnp.ones((), bf16), jnp.zeros((), bf16)
-    first = chunk[0] * (2 * NB)
-    if is_first:
+    if mass is None:
         total[...] = jnp.zeros(total.shape, f32)
     else:
         total[...] = refs[0][...]
-
-    def product(g):
-        cell = flat(order[pl.ds(pl.multiple_of(first + g * 8, 8), 8), :])
-        value = flat(lse[pl.ds(pl.multiple_of(g * 8, 8), 8), :])
-        column = lax.rem(cell // 128, 256).astype(f32).astype(bf16)
-        row = (cell // 32768 * 128 + lax.rem(cell, 128)).astype(f32).astype(bf16)
-        big = value.astype(bf16)
-        small = (value - big.astype(f32)).astype(bf16)
-        match = number == row
-        left = jnp.concatenate([jnp.where(match, big, zero), jnp.where(match, small, zero)], axis=0)
-        right = jnp.where(number == column, one, zero)
-        return lax.dot_general(left, right, NT, preferred_element_type=f32)
-
-    def step(g, carry):
-        total[...] += sum(product(g * SCATTER + u) for u in range(SCATTER))
-        return carry
-
-    lax.fori_loop(0, NB // 4 // SCATTER, step, 0)
+    for k, lse in enumerate((first_lse, second_lse)):
+        first = chunk[k] * (2 * NB)
+
+        def product(g):
+            cell = flat(order[pl.ds(pl.multiple_of(first + g * 8, 8), 8), :])
+            value = flat(lse[pl.ds(pl.multiple_of(g * 8, 8), 8), :])
+            column = lax.rem(cell // 128, 256).astype(f32).astype(bf16)
+            row = ((cell // (SRC // 2) - half) * 128 + lax.rem(cell, 128)).astype(f32).astype(bf16)
+            big = value.astype(bf16)
+            small = (value - big.astype(f32)).astype(bf16)
+            match = number[0:128] == row
+            left = jnp.concatenate([jnp.where(match, big, zero), jnp.where(match, small, zero)], axis=0)
+            right = jnp.where(number == column, one, zero)
+            return lax.dot_general(left, right, NT, preferred_element_type=f32)
+
+        def step(g, carry):
+            total[...] += sum(product(g * SCATTER + u) for u in range(SCATTER))
+            return carry
+
+        lax.fori_loop(0, NB // 4 // SCATTER, step, 0)
     if mass is None:
         out[...] = total[...]
         return
-    for half in range(2):
-        for side in range(2):
-            here, rows = slice(side * 128, side * 128 + 128), half * 128
-            both = total[rows : rows + 128, here] + total[256 + rows : 384 + rows, here]
-            here = slice(half * 256 + side * 128, half * 256 + side * 128 + 128)
-            out[here, :] = 0.1 * mass[here, :] - (0.1 * LN2) * both.T
+    base = half * 256
+    for side in range(2):
+        here = slice(side * 128, side * 128 + 128)
+        both = total[0:128, here] + total[128:256, here]
+        weight = mass[pl.ds(pl.multiple_of(base + side * 128, 128), 128), :]
+        out[here, :] = 0.1 * weight - (0.1 * LN2) * both.T
 
 
 def last_scatter_kernel(mass, *refs):
-    scatter_kernel(False, mass, *refs)
+    scatter_kernel(mass, *refs)
 
 
 def final_kernel(*refs):
-    order, mass, potential, out = refs[4:]
+    order, mass, potential, own, other, source_out, out = refs[4:]
+    half = lax.rem(lax.axis_index("col") // Y, 2)
+    source_out[pl.ds(pl.multiple_of(half * 256, 256), 256), :] = own[...]
+    source_out[pl.ds(pl.multiple_of(256 - half * 256, 256), 256), :] = other[...]
     lse = merged([ref[...] for ref in refs[:4]])
     total = jnp.zeros((TGT // 128, 256), f32)
     for g in range(TGT // 1024):
@@ -515,49 +520,51 @@
 
     order_rows = source_order.reshape(SRC // 128, 128)
     cost = dict(flops=2 * 512 * 256 * CHUNK, nbytes=2**20)
-    totals = shape((512, 256), f32)
-    keep = [pltpu.VMEM((512, 256), f32)]
-
-    def piece(d, before=None):
-        chunk = lax.rem(y + Y - d, Y).reshape(1)
-        kernel = functools.partial(scatter_kernel, before is None, None)
-        return call(
-            kernel, f"source_scatter_{d}", totals, [vmem()] * 2 + [smem()] + [vmem()] * (before is not None), keep, **cost
-        )(order_rows, lses[d], chunk, *([] if before is None else [before]))
+    keep = [pltpu.VMEM((256, 256), f32)]
+    chunks = lax.rem(y + Y - jnp.arange(Y, dtype=jnp.int32), Y)
+
+    def merge(name, parts):
+        return call(merge_kernel, name, shape((2 * TB, 128), f32), [vmem()] * len(parts), [])(*parts)
 
     own = [target_partial[0 : 2 * TB]] + [
         lax.ppermute(target_partial[2 * d * TB : 2 * (d + 1) * TB], "col", y_shift(-d)) for d in range(1, Y)
     ]
-    scattered = piece(0)
+    scattered = call(
+        functools.partial(scatter_kernel, None),
+        "source_scatter_0",
+        shape((256, 256), f32),
+        [vmem()] * 3 + [smem()],
+        keep,
+        **cost,
+    )(order_rows, lses[0], lses[1], chunks[0:2])
     own, scattered = lax.optimization_barrier((own, scattered))
-    merge = lambda name, parts: call(merge_kernel, name, shape((2 * TB, 128), f32), [vmem()] * len(parts), [])(*parts)
     own = merge("col_merge_y", own)
     own = [own, lax.ppermute(own, "row", row_pair())]
-    scattered = piece(1, scattered)
-    own, scattered = lax.optimization_barrier((own, scattered))
+    mine = call(
+        last_scatter_kernel,
+        "source_scatter_1",
+        shape((SRC // 256, 128), f32),
+        [vmem()] * 4 + [smem(), vmem()],
+        keep,
+        **cost,
+    )(mass, order_rows, lses[2], lses[3], chunks[2:4], scattered)
+    own, mine = lax.optimization_barrier((own, mine))
+    other = lax.ppermute(mine, "col", z_pair())
     own = merge("col_merge_core", own)
     own = [own] + [lax.ppermute(own, "row", row_shift(d)) for d in (2, 4, 6)]
-    scattered = piece(2, scattered)
-    source_update = call(
-        last_scatter_kernel,
-        "source_scatter_3",
-        shape((SRC // 128, 128), f32),
-        [vmem()] * 3 + [smem(), vmem()],
-        keep,
-        **cost,
-    )(mass, order_rows, lses[3], lax.rem(y + Y - 3, Y).reshape(1), scattered)
-    own, source_update = lax.optimization_barrier((own, source_update))
-    target_update = call(
+    source_update, target_update = call(
         final_kernel,
         "target_scatter",
-        shape((TGT // 128, 128), f32),
-        [vmem()] * 7,
+        [shape((SRC // 128, 128), f32), shape((TGT // 128, 128), f32)],
+        [vmem()] * 9,
         [],
     )(
         *own,
         target_order.reshape(TGT // 128, 128),
         target_mass.reshape(TGT // 128, 128),
         target_potential.reshape(TGT // 128, 128),
+        mine,
+        other,
     )
     return (source_update.reshape(SRC), target_update.reshape(TGT))
 

time: 122 us -> 112 us (0.918); the launches traced: 124 us -> 110 us
  starting transfers between devices: 43.3 us -> 33.6 us
  Pallas kernels: 74.6 us -> 65.3 us
  waiting for transfers between devices: 3.97 us -> 9.01 us
    pallas_call x7 -> x5, Pallas kernels: 21.2 us -> 12.8 us  [the longest x1 5.93 us: body(): call(last_scatter_kernel, 'source_scatter_1', shape((SRC // 256, 128), f3...]
    ppermute x3, starting transfers between devices: 8.14 us -> 3.48 us  [body(): own = [own] + [lax.ppermute(own, 'row', row_shift(d)) for d in (2, 4, 6)]]
    ppermute x3, waiting for transfers between devices: 1.33 us -> 4.2 us  [body(): lax.ppermute(partial, 'col', z_shift(d))]
    ppermute x1, starting transfers between devices: 2.1 us -> 0.09 us  [body(): partials = [lse, lax.ppermute(lse, 'col', z_pair())]]
    ppermute x3, waiting for transfers between devices: 0.01 us -> 1.75 us  [body(): own = [own] + [lax.ppermute(own, 'row', row_shift(d)) for d in (2, 4, 6)]]
    ppermute x3, starting transfers between devices: 5.5 us -> 3.83 us  [body(): lses = [lse] + [lax.ppermute(lse, 'col', y_shift(d)) for d in range(1, Y)]]
  transfers between devices with their start and end apart: 17 -> 18, of which waited for: 2 -> 6; matrix products, arithmetic and copies ran while one was open for 0% -> 0% of each run, Pallas kernels for 45% -> 42%
where the time goes in v3:
time: 112 us; the launch traced here: 110 us
  Pallas kernels  65.3 us (58%)
  starting transfers between devices  33.6 us (30%)
  waiting for transfers between devices  9.01 us (8%)
  between operations  1.48 us (1%)
    pallas_call x1, Pallas kernels, body(): call(gather_kernel, 'source_gather', shape((CHUNK, 128), bf16), [anywhere...  22.5 us
    pallas_call x1, Pallas kernels, body(): call(row_kernel, 'row_pass', [shape((2 * NB, 128), f32), shape((Y * TGT,...  12.9 us
    pallas_call x1, Pallas kernels, body(): call(col_kernel, 'col_pass', shape((2 * Y * TB, 128), f32), [anywhere(),...  12.4 us
    ppermute x3, starting transfers between devices, body(): lax.ppermute(partial, 'col', z_shift(d))  11.7 us
    ppermute x1, starting transfers between devices, body(): own = [own, lax.ppermute(own, 'row', row_pair())]  7.54 us
    pallas_call x1, Pallas kernels, body(): call(last_scatter_kernel, 'source_scatter_1', shape((SRC // 256, 128), f3...  5.93 us
    pallas_call x1, Pallas kernels, body(): call(functools.partial(scatter_kernel, None), 'source_scatter_0', shape((...  5.83 us
    ppermute x3, starting transfers between devices, body(): lax.ppermute(pack, 'col', y_shift(d))  4.68 us
  transfers between devices with their start and end apart: 18, of which 6 were waited for; matrix products, arithmetic and copies ran while one was open for 0% of the time, Pallas kernels for 42%

profile of v3, /device:TPU:1, one launch (start us, length us, event | category | flops | bytes accessed | tf_op | source)
XLA Modules:
  0.0 110.0 jit_solution(18427748109162452713)
XLA Ops:
  1.3 4.6 %target_gather.1.p0 = f32[40,2048]{1,0:T(8,128)} custom-call(bf16[32,2048]{1,0:T(8,128)(2,1)} %refs_0_.1, s32[1,2048]{1,0:T(1,128)} %refs_1_.1, f32[1,2048]{1,0:T(1,128)} %bitcast.11, s32[1,256]{1,0:T(1,128)} %bitcast.20, s32[1,256]{1,0:T(1,128)} %bitcast.21, s32[1,1]{1,0:T(1,128)S(6)} %copy.12.refs_5_), custom_call_target="tpu_custom_call" | custom-call | flops 402653184 | tf_op jit(solution)/shard_map/target_gather/pallas_call | solution.py:429
  5.9 3.6 %collective-permute-start.2 = (f32[40,2048]{1,0:T(8,128)}, f32[40,2048]{1,0:T(8,128)S(1)}, u32[]{:S(2)}, u32[]{:S(2)}) collective-permute-start(f32[40,2048]{1,0:T(8,128)} %target_gather.1.p0), channel_id=1, source_target_pairs={{0,3},{1,0},{2,1},{3,2},{4,7},{5,4},{6,5},{7,6},{8,11},{9,8},{10,9... | collective-permute-start | bytes 983048 | tf_op jit(solution)/shard_map/ppermute | solution.py:453
  9.9 0.7 collective-permute-start
  10.6 22.5 %source_gather.1.source_all = bf16[16384,128]{1,0:T(8,128)(2,1)} custom-call(bf16[32,65536]{1,0:T(8,128)(2,1)} %coords_all.1, f32[512,128]{1,0:T(8,128)} %bitcast.14, s32[1,65536]{1,0:T(1,128)} %order_all.1), custom_call_target="tpu_custom_call" | custom-call | flops 20000000000 | bytes 67108864 | tf_op jit(solution)/shard_map/source_gather/pallas_call | solution.py:455
  33.6 12.9 %row_pass.1 = (f32[128,128]{1,0:T(8,128)S(1)}, bf16[8192,128]{1,0:T(8,128)(2,1)S(1)}) custom-call(bf16[16384,128]{1,0:T(8,128)(2,1)} %source_gather.1.source_all, f32[40,2048]{1,0:T(8,128)S(1)} %copy-done, f32[40,2048]{1,0:T(8,128)S(1)} %collective-permute-done.p1, f32[40,2048]{1,0:T(8,128)S(1)} %collective-permute-done.1.p2, ...), custom_call_target="tpu_custom_call" | custom-call | tf_op jit(solution)/shard_map/row_pass/pallas_call | solution.py:481
  46.4 4.2 %collective-permute-start.3 = (f32[128,128]{1,0:T(8,128)S(1)}, f32[128,128]{1,0:T(8,128)S(1)}, u32[]{:S(2)}, u32[]{:S(2)}) collective-permute-start(f32[128,128]{1,0:T(8,128)S(1)} %get-tuple-element.15.refs_0_), channel_id=1, source_target_pairs={{0,8},{1,9},{2,10},{3,11},{4,12},{5,13},{6,14},{7,15},{8,16},{9,17... | collective-permute-start | bytes 196616 | tf_op jit(solution)/shard_map/ppermute | solution.py:498
  50.7 6.3 %collective-permute-start.4 = (f32[128,128]{1,0:T(8,128)S(1)}, f32[128,128]{1,0:T(8,128)S(1)}, u32[]{:S(2)}, u32[]{:S(2)}) collective-permute-start(f32[128,128]{1,0:T(8,128)S(1)} %get-tuple-element.15.refs_0_), channel_id=1, source_target_pairs={{0,16},{1,17},{2,18},{3,19},{4,20},{5,21},{6,22},{7,23},{8,24},{9,... | collective-permute-start | bytes 196616 | tf_op jit(solution)/shard_map/ppermute | solution.py:498
  57.0 1.2 %collective-permute-start.5 = (f32[128,128]{1,0:T(8,128)S(1)}, f32[128,128]{1,0:T(8,128)S(1)}, u32[]{:S(2)}, u32[]{:S(2)}) collective-permute-start(f32[128,128]{1,0:T(8,128)S(1)} %get-tuple-element.15.refs_0_), channel_id=1, source_target_pairs={{0,24},{1,25},{2,26},{3,27},{4,28},{5,29},{6,30},{7,31},{8,0},{9,1... | collective-permute-start | bytes 196616 | tf_op jit(solution)/shard_map/ppermute | solution.py:498
  58.2 3.2 %collective-permute-done.4.refs_2_ = f32[128,128]{1,0:T(8,128)S(1)} collective-permute-done((f32[128,128]{1,0:T(8,128)S(1)}, f32[128,128]{1,0:T(8,128)S(1)}, u32[]{:S(2)}, u32[]{:S(2)}) %collective-permute-start.4) | collective-permute-done | bytes 65568 | tf_op jit(solution)/shard_map/ppermute | solution.py:498
  61.4 1.0 collective-permute-done.5.refs_3_
  62.6 3.0 %collective-permute-done.6.refs_1_ = f32[128,128]{1,0:T(8,128)S(1)} collective-permute-done((f32[128,128]{1,0:T(8,128)S(1)}, f32[128,128]{1,0:T(8,128)S(1)}, u32[]{:S(2)}, u32[]{:S(2)}) %collective-permute-start.6) | collective-permute-done | bytes 65568 | tf_op jit(solution)/shard_map/ppermute | solution.py:500
  65.7 1.1 %collective-permute-start.10 = (f32[128,128]{1,0:T(8,128)S(1)}, f32[128,128]{1,0:T(8,128)S(1)}, u32[]{:S(2)}, u32[]{:S(2)}) collective-permute-start(f32[128,128]{1,0:T(8,128)S(1)} %row_merge_two.1.lse.first_lse), channel_id=1, source_target_pairs={{0,1},{1,2},{2,3},{3,0},{4,5},{5,6},{6,7},{7,4},{8,9},{9,10},{10,1... | collective-permute-start | bytes 196616 | tf_op jit(solution)/shard_map/ppermute | solution.py:502
  66.8 1.0 collective-permute-start.12
  67.8 1.7 %collective-permute-start.13 = (f32[128,128]{1,0:T(8,128)S(1)}, f32[128,128]{1,0:T(8,128)S(1)}, u32[]{:S(2)}, u32[]{:S(2)}) collective-permute-start(f32[128,128]{1,0:T(8,128)S(1)} %row_merge_two.1.lse.first_lse), channel_id=1, source_target_pairs={{0,3},{1,0},{2,1},{3,2},{4,7},{5,4},{6,5},{7,6},{8,11},{9,8},{10,9... | collective-permute-start | bytes 196616 | tf_op jit(solution)/shard_map/ppermute | solution.py:502
  69.5 12.4 %col_pass.1 = f32[64,128]{1,0:T(8,128)S(1)} custom-call(bf16[16384,128]{1,0:T(8,128)(2,1)} %source_gather.1.source_all, bf16[8192,128]{1,0:T(8,128)(2,1)S(1)} %get-tuple-element.14.late_all, f32[128,128]{1,0:T(8,128)S(1)} %row_merge_two.1.lse.first_lse, s32[4,256]{1,0:T(4,128)S(1)} %get-tuple-element.31.codes, s32[4]{0:T(128)S(1)} %get-tuple-element.30.counts), custom_call_target="tpu_custom_call" | custom-call | flops 20000000000 | tf_op jit(solution)/shard_map/col_pass/pallas_call | solution.py:504
  82.0 1.5 %collective-permute-start.8 = (f32[16,128]{1,0:T(8,128)S(1)}, f32[16,128]{1,0:T(8,128)S(1)}, u32[]{:S(2)}, u32[]{:S(2)}) collective-permute-start(f32[16,128]{1,0:T(8,128)S(1)} %get-tuple-element.27), channel_id=1, source_target_pairs={{0,2},{1,3},{2,0},{3,1},{4,6},{5,7},{6,4},{7,5},{8,10},{9,11},{10,... | collective-permute-start | bytes 24584 | tf_op jit(solution)/shard_map/ppermute | solution.py:530
  83.5 0.6 collective-permute-start.9
  84.2 5.8 %source_scatter_0.1.refs_4_ = f32[256,256]{1,0:T(8,128)S(1)} custom-call(s32[512,128]{1,0:T(8,128)S(1)} %bitcast.16, f32[128,128]{1,0:T(8,128)S(1)} %row_merge_two.1.lse.first_lse, f32[128,128]{1,0:T(8,128)S(1)} %collective-permute-done.10.second_lse, s32[2]{0:T(128)S(1)} %get-tuple-element.33.chunk), custom_call_target="tpu_custom_call" | custom-call | flops 4294967296 | bytes 1048576 | tf_op jit(solution)/shard_map/source_scatter_0/pallas_call | solution.py:532
  90.0 7.5 %collective-permute-start.11 = (f32[16,128]{1,0:T(8,128)S(1)}, f32[16,128]{1,0:T(8,128)S(1)}, u32[]{:S(2)}, u32[]{:S(2)}) collective-permute-start(f32[16,128]{1,0:T(8,128)S(1)} %col_merge_y.1.refs_0_), channel_id=1, source_target_pairs={{0,32},{32,0},{64,96},{96,64},{128,160},{160,128},{192,224},{224,1... | collective-permute-start | bytes 24584 | tf_op jit(solution)/shard_map/ppermute | solution.py:542
  97.6 5.9 %source_scatter_1.1.refs_7_ = f32[256,128]{1,0:T(8,128)S(1)} custom-call(f32[512,128]{1,0:T(8,128)S(1)} %bitcast.15, s32[512,128]{1,0:T(8,128)S(1)} %bitcast.17, f32[128,128]{1,0:T(8,128)S(1)} %collective-permute-done.12.refs_1_, f32[128,128]{1,0:T(8,128)S(1)} %collective-permute-done.13.refs_2_, s32[2]{0:T(128)S(1)} %get-tuple-element.32.refs_3_, ...), custom_call_target="tpu_custom_call" | custom-call | flops 4294967296 | bytes 1048576 | tf_op jit(solution)/shard_map/source_scatter_1/pallas_call | solution.py:543
  103.8 2.4 %collective-permute-start.15 = (f32[16,128]{1,0:T(8,128)S(1)}, f32[16,128]{1,0:T(8,128)S(1)}, u32[]{:S(2)}, u32[]{:S(2)}) collective-permute-start(f32[16,128]{1,0:T(8,128)S(1)} %col_merge_core.1.refs_0_), channel_id=1, source_target_pairs={{0,128},{32,160},{64,192},{96,224},{128,0},{160,32},{192,64},{224,... | collective-permute-start | bytes 24584 | tf_op jit(solution)/shard_map/ppermute | solution.py:554
  106.1 1.0 collective-permute-start.16
  107.9 1.1 collective-permute-done.16.refs_3_
  109.0 1.0 target_scatter.1
  (43 shorter events, 2.1 us)
Async XLA Ops:
  5.9 27.3 %collective-permute-start.2 = (f32[40,2048]{1,0:T(8,128)}, f32[40,2048]{1,0:T(8,128)S(1)}, u32[]{:S(2)}, u32[]{:S(2)}) collective-permute-start(f32[40,2048]{1,0:T(8,128)} %target_gather.1.p0), channel_id=1, source_target_pairs={{0,3},{1,0},{2,1},{3,2},{4,7},{5,4},{6,5},{7,6},{8,11},{9,8},{10,9... | collective-permute-start | bytes 983048 | tf_op jit(solution)/shard_map/ppermute | solution.py:453
  9.5 23.8 %collective-permute-start.1 = (f32[40,2048]{1,0:T(8,128)}, f32[40,2048]{1,0:T(8,128)S(1)}, u32[]{:S(2)}, u32[]{:S(2)}) collective-permute-start(f32[40,2048]{1,0:T(8,128)} %target_gather.1.p0), channel_id=1, source_target_pairs={{0,2},{1,3},{2,0},{3,1},{4,6},{5,7},{6,4},{7,5},{8,10},{9,11},{10,... | collective-permute-start | bytes 983048 | tf_op jit(solution)/shard_map/ppermute | solution.py:453
  9.9 23.5 %collective-permute-start = (f32[40,2048]{1,0:T(8,128)}, f32[40,2048]{1,0:T(8,128)S(1)}, u32[]{:S(2)}, u32[]{:S(2)}) collective-permute-start(f32[40,2048]{1,0:T(8,128)} %target_gather.1.p0), channel_id=1, source_target_pairs={{0,1},{1,2},{2,3},{3,0},{4,5},{5,6},{6,7},{7,4},{8,9},{9,10},{10,1... | collective-permute-start | bytes 983048 | tf_op jit(solution)/shard_map/ppermute | solution.py:453
  10.6 22.5 %copy-start = (f32[40,2048]{1,0:T(8,128)S(1)}, f32[40,2048]{1,0:T(8,128)}, u32[]{:S(2)}) copy-start(f32[40,2048]{1,0:T(8,128)} %target_gather.1.p0) | copy-start | bytes 983044
  46.4 11.8 %collective-permute-start.3 = (f32[128,128]{1,0:T(8,128)S(1)}, f32[128,128]{1,0:T(8,128)S(1)}, u32[]{:S(2)}, u32[]{:S(2)}) collective-permute-start(f32[128,128]{1,0:T(8,128)S(1)} %get-tuple-element.15.refs_0_), channel_id=1, source_target_pairs={{0,8},{1,9},{2,10},{3,11},{4,12},{5,13},{6,14},{7,15},{8,16},{9,17... | collective-permute-start | bytes 196616 | tf_op jit(solution)/shard_map/ppermute | solution.py:498
  50.7 10.7 %collective-permute-start.4 = (f32[128,128]{1,0:T(8,128)S(1)}, f32[128,128]{1,0:T(8,128)S(1)}, u32[]{:S(2)}, u32[]{:S(2)}) collective-permute-start(f32[128,128]{1,0:T(8,128)S(1)} %get-tuple-element.15.refs_0_), channel_id=1, source_target_pairs={{0,16},{1,17},{2,18},{3,19},{4,20},{5,21},{6,22},{7,23},{8,24},{9,... | collective-permute-start | bytes 196616 | tf_op jit(solution)/shard_map/ppermute | solution.py:498
  57.0 5.4 %collective-permute-start.5 = (f32[128,128]{1,0:T(8,128)S(1)}, f32[128,128]{1,0:T(8,128)S(1)}, u32[]{:S(2)}, u32[]{:S(2)}) collective-permute-start(f32[128,128]{1,0:T(8,128)S(1)} %get-tuple-element.15.refs_0_), channel_id=1, source_target_pairs={{0,24},{1,25},{2,26},{3,27},{4,28},{5,29},{6,30},{7,31},{8,0},{9,1... | collective-permute-start | bytes 196616 | tf_op jit(solution)/shard_map/ppermute | solution.py:498
  62.4 3.2 %collective-permute-start.6 = (f32[128,128]{1,0:T(8,128)S(1)}, f32[128,128]{1,0:T(8,128)S(1)}, u32[]{:S(2)}, u32[]{:S(2)}) collective-permute-start(f32[128,128]{1,0:T(8,128)S(1)} %row_merge_four.1.refs_0_), channel_id=1, source_target_pairs={{0,4},{1,5},{2,6},{3,7},{4,0},{5,1},{6,2},{7,3},{8,12},{9,13},{10,... | collective-permute-start | bytes 196616 | tf_op jit(solution)/shard_map/ppermute | solution.py:500
  65.7 17.8 %collective-permute-start.10 = (f32[128,128]{1,0:T(8,128)S(1)}, f32[128,128]{1,0:T(8,128)S(1)}, u32[]{:S(2)}, u32[]{:S(2)}) collective-permute-start(f32[128,128]{1,0:T(8,128)S(1)} %row_merge_two.1.lse.first_lse), channel_id=1, source_target_pairs={{0,1},{1,2},{2,3},{3,0},{4,5},{5,6},{6,7},{7,4},{8,9},{9,10},{10,1... | collective-permute-start | bytes 196616 | tf_op jit(solution)/shard_map/ppermute | solution.py:502
  66.8 30.8 %collective-permute-start.12 = (f32[128,128]{1,0:T(8,128)S(1)}, f32[128,128]{1,0:T(8,128)S(1)}, u32[]{:S(2)}, u32[]{:S(2)}) collective-permute-start(f32[128,128]{1,0:T(8,128)S(1)} %row_merge_two.1.lse.first_lse), channel_id=1, source_target_pairs={{0,2},{1,3},{2,0},{3,1},{4,6},{5,7},{6,4},{7,5},{8,10},{9,11},{10,... | collective-permute-start | bytes 196616 | tf_op jit(solution)/shard_map/ppermute | solution.py:502
  67.8 29.8 %collective-permute-start.13 = (f32[128,128]{1,0:T(8,128)S(1)}, f32[128,128]{1,0:T(8,128)S(1)}, u32[]{:S(2)}, u32[]{:S(2)}) collective-permute-start(f32[128,128]{1,0:T(8,128)S(1)} %row_merge_two.1.lse.first_lse), channel_id=1, source_target_pairs={{0,3},{1,0},{2,1},{3,2},{4,7},{5,4},{6,5},{7,6},{8,11},{9,8},{10,9... | collective-permute-start | bytes 196616 | tf_op jit(solution)/shard_map/ppermute | solution.py:502
  69.5 14.6 %copy-start.5 = (s32[1,65536]{1,0:T(1,128)S(1)}, s32[1,65536]{1,0:T(1,128)}, u32[]{:S(2)}) copy-start(s32[1,65536]{1,0:T(1,128)} %order_all.1) | copy-start | bytes 786436
  82.0 8.0 %collective-permute-start.7 = (f32[16,128]{1,0:T(8,128)S(1)}, f32[16,128]{1,0:T(8,128)S(1)}, u32[]{:S(2)}, u32[]{:S(2)}) collective-permute-start(f32[16,128]{1,0:T(8,128)S(1)} %get-tuple-element.28), channel_id=1, source_target_pairs={{0,3},{1,0},{2,1},{3,2},{4,7},{5,4},{6,5},{7,6},{8,11},{9,8},{10,9... | collective-permute-start | bytes 24584 | tf_op jit(solution)/shard_map/ppermute | solution.py:530
  82.0 8.0 %collective-permute-start.8 = (f32[16,128]{1,0:T(8,128)S(1)}, f32[16,128]{1,0:T(8,128)S(1)}, u32[]{:S(2)}, u32[]{:S(2)}) collective-permute-start(f32[16,128]{1,0:T(8,128)S(1)} %get-tuple-element.27), channel_id=1, source_target_pairs={{0,2},{1,3},{2,0},{3,1},{4,6},{5,7},{6,4},{7,5},{8,10},{9,11},{10,... | collective-permute-start | bytes 24584 | tf_op jit(solution)/shard_map/ppermute | solution.py:530
  83.5 6.5 %collective-permute-start.9 = (f32[16,128]{1,0:T(8,128)S(1)}, f32[16,128]{1,0:T(8,128)S(1)}, u32[]{:S(2)}, u32[]{:S(2)}) collective-permute-start(f32[16,128]{1,0:T(8,128)S(1)} %get-tuple-element.26), channel_id=1, source_target_pairs={{0,1},{1,2},{2,3},{3,0},{4,5},{5,6},{6,7},{7,4},{8,9},{9,10},{10,1... | collective-permute-start | bytes 24584 | tf_op jit(solution)/shard_map/ppermute | solution.py:530
  84.1 13.4 %copy-start.4 = (f32[65536]{0:T(1024)S(1)}, f32[65536]{0:T(1024)}, u32[]{:S(2)}) copy-start(f32[65536]{0:T(1024)} %param.14) | copy-start | bytes 786436
  90.0 13.5 %collective-permute-start.11 = (f32[16,128]{1,0:T(8,128)S(1)}, f32[16,128]{1,0:T(8,128)S(1)}, u32[]{:S(2)}, u32[]{:S(2)}) collective-permute-start(f32[16,128]{1,0:T(8,128)S(1)} %col_merge_y.1.refs_0_), channel_id=1, source_target_pairs={{0,32},{32,0},{64,96},{96,64},{128,160},{160,128},{192,224},{224,1... | collective-permute-start | bytes 24584 | tf_op jit(solution)/shard_map/ppermute | solution.py:542
  97.6 11.4 %copy-start.1 = (s32[1,2048]{1,0:T(1,128)S(1)}, s32[1,2048]{1,0:T(1,128)}, u32[]{:S(2)}) copy-start(s32[1,2048]{1,0:T(1,128)} %refs_1_.1) | copy-start | bytes 24580
  97.6 11.3 %copy-start.2 = (f32[2048]{0:T(1024)S(1)}, f32[2048]{0:T(1024)}, u32[]{:S(2)}) copy-start(f32[2048]{0:T(1024)} %param.16) | copy-start | bytes 24580
  97.6 11.3 %copy-start.3 = (f32[2048]{0:T(1024)S(1)}, f32[2048]{0:T(1024)}, u32[]{:S(2)}) copy-start(f32[2048]{0:T(1024)} %param.15) | copy-start | bytes 24580
  103.6 5.4 %collective-permute-start.17 = (f32[256,128]{1,0:T(8,128)S(1)}, f32[256,128]{1,0:T(8,128)S(1)}, u32[]{:S(2)}, u32[]{:S(2)}) collective-permute-start(f32[256,128]{1,0:T(8,128)S(1)} %source_scatter_1.1.refs_7_), channel_id=1, source_target_pairs={{0,4},{1,5},{2,6},{3,7},{4,0},{5,1},{6,2},{7,3},{8,12},{9,13},{10,... | collective-permute-start | bytes 393224 | tf_op jit(solution)/shard_map/ppermute | solution.py:552
  103.7 3.8 %collective-permute-start.14 = (f32[16,128]{1,0:T(8,128)S(1)}, f32[16,128]{1,0:T(8,128)S(1)}, u32[]{:S(2)}, u32[]{:S(2)}) collective-permute-start(f32[16,128]{1,0:T(8,128)S(1)} %col_merge_core.1.refs_0_), channel_id=1, source_target_pairs={{0,64},{32,96},{64,128},{96,160},{128,192},{160,224},{192,0},{224,... | collective-permute-start | bytes 24584 | tf_op jit(solution)/shard_map/ppermute | solution.py:554
  103.8 4.1 %collective-permute-start.15 = (f32[16,128]{1,0:T(8,128)S(1)}, f32[16,128]{1,0:T(8,128)S(1)}, u32[]{:S(2)}, u32[]{:S(2)}) collective-permute-start(f32[16,128]{1,0:T(8,128)S(1)} %col_merge_core.1.refs_0_), channel_id=1, source_target_pairs={{0,128},{32,160},{64,192},{96,224},{128,0},{160,32},{192,64},{224,... | collective-permute-start | bytes 24584 | tf_op jit(solution)/shard_map/ppermute | solution.py:554
  106.1 2.8 %collective-permute-start.16 = (f32[16,128]{1,0:T(8,128)S(1)}, f32[16,128]{1,0:T(8,128)S(1)}, u32[]{:S(2)}, u32[]{:S(2)}) collective-permute-start(f32[16,128]{1,0:T(8,128)S(1)} %col_merge_core.1.refs_0_), channel_id=1, source_target_pairs={{0,192},{32,224},{64,0},{96,32},{128,64},{160,96},{192,128},{224,1... | collective-permute-start | bytes 24584 | tf_op jit(solution)/shard_map/ppermute | solution.py:554

commit v4 on v3

--- a/solution.py
+++ b/solution.py
@@ -20,8 +20,9 @@
 TB = TGT // BLK
 CAP = 256
 UNROLL = 16
-SCATTER = 8
-BUILD = 32
+SCATTER = 16
+BUILD = 64
+FILL = 32
 LOADS = 4
 STORES = 4
 PACK = 40
@@ -91,7 +92,7 @@
     left[32:48, :] = jnp.concatenate([part, jnp.zeros((8, TGT), f32)], axis=0).astype(bf16)
     number = iota((TGT, BLK), 0)
 
-    def one_block(b, carry):
+    def one_block(b):
         span = pl.ds(pl.multiple_of(b * BLK, BLK), BLK)
         picked = indicator(number == order[:, span])
         got = jnp.dot(left[...], picked, preferred_element_type=f32)
@@ -100,9 +101,13 @@
         a = (v - jnp.sum(y * y, axis=0, keepdims=True) * (1.0 / PC)) * KAPPA
         out[0:32, span] = y
         out[32:40, span] = jnp.broadcast_to(a, (8, BLK))
+
+    def two_blocks(g, carry):
+        one_block(2 * g)
+        one_block(2 * g + 1)
         return carry
 
-    lax.fori_loop(0, TB, one_block, 0)
+    lax.fori_loop(0, TB // 2, two_blocks, 0)
 
     src = which_source[...]
     used = iota((1, CAP), 1) < count[0, 0]
@@ -243,7 +248,7 @@
     sub8 = iota((8, 128), 0)
     for d, pack in enumerate((p0, p1, p2, p3)):
 
-        def build(b, carry):
+        def build(b):
             span = pl.ds(pl.multiple_of(b * 128, 128), 128)
             h, m, l = three(pack[0:32, span] * (KAPPA / 16.0))
             ah, am, al = three(jnp.broadcast_to(pack[32:33, span], (8, 128)))
@@ -253,9 +258,13 @@
             place = pl.ds(pl.multiple_of(d * TGT + b * 128, 128), 128)
             early[place, :] = rows
             late[place, :] = rows + turned
+
+        def several(g, carry):
+            for u in range(16):
+                build(g * 16 + u)
             return carry
 
-        lax.fori_loop(0, TGT // 128, build, 0)
+        lax.fori_loop(0, TGT // 2048, several, 0)
 
     store = pltpu.make_async_copy(late, late_all, sem.at[1])
     store.start()
@@ -294,18 +303,18 @@
     sub8 = iota((8, 128), 0)
 
     def fill(g, carry):
-        for u in range(4):
-            row = -lse[pl.ds(g * 4 + u, 1), :]
+        for u in range(FILL):
+            row = -lse[pl.ds(g * FILL + u, 1), :]
             h, m, l = three(jnp.broadcast_to(row, (8, 128)))
             part = jnp.where(sub8 == 1, h, jnp.where(sub8 == 2, m, jnp.where(sub8 == 3, l, 0.0)))
             rows = jnp.concatenate([jnp.zeros((104, 128), f32), part, jnp.zeros((16, 128), f32)], axis=0)
-            span = pl.ds(pl.multiple_of((g * 4 + u) * 128, 128), 128)
+            span = pl.ds(pl.multiple_of((g * FILL + u) * 128, 128), 128)
             filled[span, :] = filled[span, :] + rows.astype(bf16).T
         return carry
 
     for k in range(LOADS):
         loads[k].wait()
-        lax.fori_loop(k * (share // 512), (k + 1) * (share // 512), fill, 0)
+        lax.fori_loop(k * (share // 128 // FILL), (k + 1) * (share // 128 // FILL), fill, 0)
     second.wait()
     partial[...] = tiles(
         lambda s, t: filled[pl.ds(pl.multiple_of(s * BLK, BLK), BLK), :],

time: 112 us -> 104 us (0.929)
  the two profiles are of different devices: /device:TPU:1 before, /device:TPU:6 now
where the time goes in v4:
time: 104 us; the launch traced here: 103 us
  Pallas kernels  57.1 us (55%)
  starting transfers between devices  32.3 us (31%)
  waiting for transfers between devices  11.4 us (11%)
  between operations  1.5 us (1%)
    pallas_call x1, Pallas kernels, body(): call(gather_kernel, 'source_gather', shape((CHUNK, 128), bf16), [anywhere...  21.9 us
    ppermute x3, starting transfers between devices, body(): lax.ppermute(partial, 'col', z_shift(d))  12.6 us
    pallas_call x1, Pallas kernels, body(): call(col_kernel, 'col_pass', shape((2 * Y * TB, 128), f32), [anywhere(),...  10.7 us
    pallas_call x1, Pallas kernels, body(): call(row_kernel, 'row_pass', [shape((2 * NB, 128), f32), shape((Y * TGT,...  9.02 us
    ppermute x3, starting transfers between devices, body(): lses = [lse] + [lax.ppermute(lse, 'col', y_shift(d)) for d in range(1, Y)]  6.03 us
    pallas_call x1, Pallas kernels, body(): call(last_scatter_kernel, 'source_scatter_1', shape((SRC // 256, 128), f3...  5.18 us
    pallas_call x1, Pallas kernels, body(): call(functools.partial(scatter_kernel, None), 'source_scatter_0', shape((...  5.11 us
    ppermute x3, waiting for transfers between devices, body(): own = [own] + [lax.ppermute(own, 'row', row_shift(d)) for d in (2, 4, 6)]  4.86 us
  transfers between devices with their start and end apart: 18, of which 5 were waited for; matrix products, arithmetic and copies ran while one was open for 0% of the time, Pallas kernels for 42%

profile of v4, /device:TPU:6, one launch (start us, length us, event | category | flops | bytes accessed | tf_op | source)
XLA Modules:
  0.0 102.9 jit_solution(4972594702367800156)
XLA Ops:
  1.3 4.1 %target_gather.1.p0 = f32[40,2048]{1,0:T(8,128)} custom-call(bf16[32,2048]{1,0:T(8,128)(2,1)} %refs_0_.1, s32[1,2048]{1,0:T(1,128)} %refs_1_.1, f32[1,2048]{1,0:T(1,128)} %bitcast.11, s32[1,256]{1,0:T(1,128)} %bitcast.20, s32[1,256]{1,0:T(1,128)} %bitcast.21, s32[1,1]{1,0:T(1,128)S(6)} %copy.12.refs_5_), custom_call_target="tpu_custom_call" | custom-call | flops 402653184 | tf_op jit(solution)/shard_map/target_gather/pallas_call | solution.py:438
  5.4 3.1 %collective-permute-start.2 = (f32[40,2048]{1,0:T(8,128)}, f32[40,2048]{1,0:T(8,128)S(1)}, u32[]{:S(2)}, u32[]{:S(2)}) collective-permute-start(f32[40,2048]{1,0:T(8,128)} %target_gather.1.p0), channel_id=1, source_target_pairs={{0,3},{1,0},{2,1},{3,2},{4,7},{5,4},{6,5},{7,6},{8,11},{9,8},{10,9... | collective-permute-start | bytes 983048 | tf_op jit(solution)/shard_map/ppermute | solution.py:462
  8.5 0.6 collective-permute-start.1
  9.1 1.0 collective-permute-start
  10.1 21.9 %source_gather.1.source_all = bf16[16384,128]{1,0:T(8,128)(2,1)} custom-call(bf16[32,65536]{1,0:T(8,128)(2,1)} %coords_all.1, f32[512,128]{1,0:T(8,128)} %bitcast.14, s32[1,65536]{1,0:T(1,128)} %order_all.1), custom_call_target="tpu_custom_call" | custom-call | flops 20000000000 | bytes 67108864 | tf_op jit(solution)/shard_map/source_gather/pallas_call | solution.py:464
  32.5 9.0 %row_pass.1 = (f32[128,128]{1,0:T(8,128)S(1)}, bf16[8192,128]{1,0:T(8,128)(2,1)S(1)}) custom-call(bf16[16384,128]{1,0:T(8,128)(2,1)} %source_gather.1.source_all, f32[40,2048]{1,0:T(8,128)S(1)} %copy-done, f32[40,2048]{1,0:T(8,128)S(1)} %collective-permute-done.p1, f32[40,2048]{1,0:T(8,128)S(1)} %collective-permute-done.1.p2, ...), custom_call_target="tpu_custom_call" | custom-call | tf_op jit(solution)/shard_map/row_pass/pallas_call | solution.py:490
  41.5 4.5 %collective-permute-start.3 = (f32[128,128]{1,0:T(8,128)S(1)}, f32[128,128]{1,0:T(8,128)S(1)}, u32[]{:S(2)}, u32[]{:S(2)}) collective-permute-start(f32[128,128]{1,0:T(8,128)S(1)} %get-tuple-element.15.refs_0_), channel_id=1, source_target_pairs={{0,8},{1,9},{2,10},{3,11},{4,12},{5,13},{6,14},{7,15},{8,16},{9,17... | collective-permute-start | bytes 196616 | tf_op jit(solution)/shard_map/ppermute | solution.py:507
  46.0 4.1 %collective-permute-start.4 = (f32[128,128]{1,0:T(8,128)S(1)}, f32[128,128]{1,0:T(8,128)S(1)}, u32[]{:S(2)}, u32[]{:S(2)}) collective-permute-start(f32[128,128]{1,0:T(8,128)S(1)} %get-tuple-element.15.refs_0_), channel_id=1, source_target_pairs={{0,16},{1,17},{2,18},{3,19},{4,20},{5,21},{6,22},{7,23},{8,24},{9,... | collective-permute-start | bytes 196616 | tf_op jit(solution)/shard_map/ppermute | solution.py:507
  50.0 4.0 %collective-permute-start.5 = (f32[128,128]{1,0:T(8,128)S(1)}, f32[128,128]{1,0:T(8,128)S(1)}, u32[]{:S(2)}, u32[]{:S(2)}) collective-permute-start(f32[128,128]{1,0:T(8,128)S(1)} %get-tuple-element.15.refs_0_), channel_id=1, source_target_pairs={{0,24},{1,25},{2,26},{3,27},{4,28},{5,29},{6,30},{7,31},{8,0},{9,1... | collective-permute-start | bytes 196616 | tf_op jit(solution)/shard_map/ppermute | solution.py:507
  54.1 2.5 %collective-permute-done.5.refs_3_ = f32[128,128]{1,0:T(8,128)S(1)} collective-permute-done((f32[128,128]{1,0:T(8,128)S(1)}, f32[128,128]{1,0:T(8,128)S(1)}, u32[]{:S(2)}, u32[]{:S(2)}) %collective-permute-start.5) | collective-permute-done | bytes 65568 | tf_op jit(solution)/shard_map/ppermute | solution.py:507
  57.1 4.0 %collective-permute-done.6.refs_1_ = f32[128,128]{1,0:T(8,128)S(1)} collective-permute-done((f32[128,128]{1,0:T(8,128)S(1)}, f32[128,128]{1,0:T(8,128)S(1)}, u32[]{:S(2)}, u32[]{:S(2)}) %collective-permute-start.6) | collective-permute-done | bytes 65568 | tf_op jit(solution)/shard_map/ppermute | solution.py:509
  61.2 2.4 %collective-permute-start.10 = (f32[128,128]{1,0:T(8,128)S(1)}, f32[128,128]{1,0:T(8,128)S(1)}, u32[]{:S(2)}, u32[]{:S(2)}) collective-permute-start(f32[128,128]{1,0:T(8,128)S(1)} %row_merge_two.1.lse.first_lse), channel_id=1, source_target_pairs={{0,1},{1,2},{2,3},{3,0},{4,5},{5,6},{6,7},{7,4},{8,9},{9,10},{10,1... | collective-permute-start | bytes 196616 | tf_op jit(solution)/shard_map/ppermute | solution.py:511
  63.5 2.0 %collective-permute-start.12 = (f32[128,128]{1,0:T(8,128)S(1)}, f32[128,128]{1,0:T(8,128)S(1)}, u32[]{:S(2)}, u32[]{:S(2)}) collective-permute-start(f32[128,128]{1,0:T(8,128)S(1)} %row_merge_two.1.lse.first_lse), channel_id=1, source_target_pairs={{0,2},{1,3},{2,0},{3,1},{4,6},{5,7},{6,4},{7,5},{8,10},{9,11},{10,... | collective-permute-start | bytes 196616 | tf_op jit(solution)/shard_map/ppermute | solution.py:511
  65.5 1.7 %collective-permute-start.13 = (f32[128,128]{1,0:T(8,128)S(1)}, f32[128,128]{1,0:T(8,128)S(1)}, u32[]{:S(2)}, u32[]{:S(2)}) collective-permute-start(f32[128,128]{1,0:T(8,128)S(1)} %row_merge_two.1.lse.first_lse), channel_id=1, source_target_pairs={{0,3},{1,0},{2,1},{3,2},{4,7},{5,4},{6,5},{7,6},{8,11},{9,8},{10,9... | collective-permute-start | bytes 196616 | tf_op jit(solution)/shard_map/ppermute | solution.py:511
  67.2 10.7 %col_pass.1 = f32[64,128]{1,0:T(8,128)S(1)} custom-call(bf16[16384,128]{1,0:T(8,128)(2,1)} %source_gather.1.source_all, bf16[8192,128]{1,0:T(8,128)(2,1)S(1)} %get-tuple-element.14.late_all, f32[128,128]{1,0:T(8,128)S(1)} %row_merge_two.1.lse.first_lse, s32[4,256]{1,0:T(4,128)S(1)} %get-tuple-element.31.codes, s32[4]{0:T(128)S(1)} %get-tuple-element.30.counts), custom_call_target="tpu_custom_call" | custom-call | flops 20000000000 | tf_op jit(solution)/shard_map/col_pass/pallas_call | solution.py:513
  77.9 0.4 collective-permute-start.7
  78.3 2.0 %collective-permute-start.8 = (f32[16,128]{1,0:T(8,128)S(1)}, f32[16,128]{1,0:T(8,128)S(1)}, u32[]{:S(2)}, u32[]{:S(2)}) collective-permute-start(f32[16,128]{1,0:T(8,128)S(1)} %get-tuple-element.27), channel_id=1, source_target_pairs={{0,2},{1,3},{2,0},{3,1},{4,6},{5,7},{6,4},{7,5},{8,10},{9,11},{10,... | collective-permute-start | bytes 24584 | tf_op jit(solution)/shard_map/ppermute | solution.py:539
  80.3 5.1 %source_scatter_0.1.refs_4_ = f32[256,256]{1,0:T(8,128)S(1)} custom-call(s32[512,128]{1,0:T(8,128)S(1)} %bitcast.16, f32[128,128]{1,0:T(8,128)S(1)} %row_merge_two.1.lse.first_lse, f32[128,128]{1,0:T(8,128)S(1)} %collective-permute-done.10.second_lse, s32[2]{0:T(128)S(1)} %get-tuple-element.33.chunk), custom_call_target="tpu_custom_call" | custom-call | flops 4294967296 | bytes 1048576 | tf_op jit(solution)/shard_map/source_scatter_0/pallas_call | solution.py:541
  85.9 5.2 %source_scatter_1.1.refs_7_ = f32[256,128]{1,0:T(8,128)S(1)} custom-call(f32[512,128]{1,0:T(8,128)S(1)} %bitcast.15, s32[512,128]{1,0:T(8,128)S(1)} %bitcast.17, f32[128,128]{1,0:T(8,128)S(1)} %collective-permute-done.12.refs_1_, f32[128,128]{1,0:T(8,128)S(1)} %collective-permute-done.13.refs_2_, s32[2]{0:T(128)S(1)} %get-tuple-element.32.refs_3_, ...), custom_call_target="tpu_custom_call" | custom-call | flops 4294967296 | bytes 1048576 | tf_op jit(solution)/shard_map/source_scatter_1/pallas_call | solution.py:552
  91.1 1.9 %collective-permute-start.17 = (f32[256,128]{1,0:T(8,128)S(1)}, f32[256,128]{1,0:T(8,128)S(1)}, u32[]{:S(2)}, u32[]{:S(2)}) collective-permute-start(f32[256,128]{1,0:T(8,128)S(1)} %source_scatter_1.1.refs_7_), channel_id=1, source_target_pairs={{0,4},{1,5},{2,6},{3,7},{4,0},{5,1},{6,2},{7,3},{8,12},{9,13},{10,... | collective-permute-start | bytes 393224 | tf_op jit(solution)/shard_map/ppermute | solution.py:561
  93.1 3.9 %collective-permute-start.15 = (f32[16,128]{1,0:T(8,128)S(1)}, f32[16,128]{1,0:T(8,128)S(1)}, u32[]{:S(2)}, u32[]{:S(2)}) collective-permute-start(f32[16,128]{1,0:T(8,128)S(1)} %col_merge_core.1.refs_0_), channel_id=1, source_target_pairs={{0,128},{32,160},{64,192},{96,224},{128,0},{160,32},{192,64},{224,... | collective-permute-start | bytes 24584 | tf_op jit(solution)/shard_map/ppermute | solution.py:563
  97.0 1.6 %collective-permute-done.15.refs_2_ = f32[16,128]{1,0:T(8,128)S(1)} collective-permute-done((f32[16,128]{1,0:T(8,128)S(1)}, f32[16,128]{1,0:T(8,128)S(1)}, u32[]{:S(2)}, u32[]{:S(2)}) %collective-permute-start.15) | collective-permute-done | bytes 8224 | tf_op jit(solution)/shard_map/ppermute | solution.py:563
  98.6 3.2 %collective-permute-done.16.refs_3_ = f32[16,128]{1,0:T(8,128)S(1)} collective-permute-done((f32[16,128]{1,0:T(8,128)S(1)}, f32[16,128]{1,0:T(8,128)S(1)}, u32[]{:S(2)}, u32[]{:S(2)}) %collective-permute-start.16) | collective-permute-done | bytes 8224 | tf_op jit(solution)/shard_map/ppermute | solution.py:563
  101.9 1.0 target_scatter.1
  (43 shorter events, 1.6 us)
Async XLA Ops:
  5.4 26.7 %collective-permute-start.2 = (f32[40,2048]{1,0:T(8,128)}, f32[40,2048]{1,0:T(8,128)S(1)}, u32[]{:S(2)}, u32[]{:S(2)}) collective-permute-start(f32[40,2048]{1,0:T(8,128)} %target_gather.1.p0), channel_id=1, source_target_pairs={{0,3},{1,0},{2,1},{3,2},{4,7},{5,4},{6,5},{7,6},{8,11},{9,8},{10,9... | collective-permute-start | bytes 983048 | tf_op jit(solution)/shard_map/ppermute | solution.py:462
  8.5 23.7 %collective-permute-start.1 = (f32[40,2048]{1,0:T(8,128)}, f32[40,2048]{1,0:T(8,128)S(1)}, u32[]{:S(2)}, u32[]{:S(2)}) collective-permute-start(f32[40,2048]{1,0:T(8,128)} %target_gather.1.p0), channel_id=1, source_target_pairs={{0,2},{1,3},{2,0},{3,1},{4,6},{5,7},{6,4},{7,5},{8,10},{9,11},{10,... | collective-permute-start | bytes 983048 | tf_op jit(solution)/shard_map/ppermute | solution.py:462
  9.1 23.1 %collective-permute-start = (f32[40,2048]{1,0:T(8,128)}, f32[40,2048]{1,0:T(8,128)S(1)}, u32[]{:S(2)}, u32[]{:S(2)}) collective-permute-start(f32[40,2048]{1,0:T(8,128)} %target_gather.1.p0), channel_id=1, source_target_pairs={{0,1},{1,2},{2,3},{3,0},{4,5},{5,6},{6,7},{7,4},{8,9},{9,10},{10,1... | collective-permute-start | bytes 983048 | tf_op jit(solution)/shard_map/ppermute | solution.py:462
  10.1 21.9 %copy-start = (f32[40,2048]{1,0:T(8,128)S(1)}, f32[40,2048]{1,0:T(8,128)}, u32[]{:S(2)}) copy-start(f32[40,2048]{1,0:T(8,128)} %target_gather.1.p0) | copy-start | bytes 983044
  41.5 12.6 %collective-permute-start.3 = (f32[128,128]{1,0:T(8,128)S(1)}, f32[128,128]{1,0:T(8,128)S(1)}, u32[]{:S(2)}, u32[]{:S(2)}) collective-permute-start(f32[128,128]{1,0:T(8,128)S(1)} %get-tuple-element.15.refs_0_), channel_id=1, source_target_pairs={{0,8},{1,9},{2,10},{3,11},{4,12},{5,13},{6,14},{7,15},{8,16},{9,17... | collective-permute-start | bytes 196616 | tf_op jit(solution)/shard_map/ppermute | solution.py:507
  46.0 8.2 %collective-permute-start.4 = (f32[128,128]{1,0:T(8,128)S(1)}, f32[128,128]{1,0:T(8,128)S(1)}, u32[]{:S(2)}, u32[]{:S(2)}) collective-permute-start(f32[128,128]{1,0:T(8,128)S(1)} %get-tuple-element.15.refs_0_), channel_id=1, source_target_pairs={{0,16},{1,17},{2,18},{3,19},{4,20},{5,21},{6,22},{7,23},{8,24},{9,... | collective-permute-start | bytes 196616 | tf_op jit(solution)/shard_map/ppermute | solution.py:507
  50.0 6.6 %collective-permute-start.5 = (f32[128,128]{1,0:T(8,128)S(1)}, f32[128,128]{1,0:T(8,128)S(1)}, u32[]{:S(2)}, u32[]{:S(2)}) collective-permute-start(f32[128,128]{1,0:T(8,128)S(1)} %get-tuple-element.15.refs_0_), channel_id=1, source_target_pairs={{0,24},{1,25},{2,26},{3,27},{4,28},{5,29},{6,30},{7,31},{8,0},{9,1... | collective-permute-start | bytes 196616 | tf_op jit(solution)/shard_map/ppermute | solution.py:507
  56.7 4.5 %collective-permute-start.6 = (f32[128,128]{1,0:T(8,128)S(1)}, f32[128,128]{1,0:T(8,128)S(1)}, u32[]{:S(2)}, u32[]{:S(2)}) collective-permute-start(f32[128,128]{1,0:T(8,128)S(1)} %row_merge_four.1.refs_0_), channel_id=1, source_target_pairs={{0,4},{1,5},{2,6},{3,7},{4,0},{5,1},{6,2},{7,3},{8,12},{9,13},{10,... | collective-permute-start | bytes 196616 | tf_op jit(solution)/shard_map/ppermute | solution.py:509
  61.2 19.1 %collective-permute-start.10 = (f32[128,128]{1,0:T(8,128)S(1)}, f32[128,128]{1,0:T(8,128)S(1)}, u32[]{:S(2)}, u32[]{:S(2)}) collective-permute-start(f32[128,128]{1,0:T(8,128)S(1)} %row_merge_two.1.lse.first_lse), channel_id=1, source_target_pairs={{0,1},{1,2},{2,3},{3,0},{4,5},{5,6},{6,7},{7,4},{8,9},{9,10},{10,1... | collective-permute-start | bytes 196616 | tf_op jit(solution)/shard_map/ppermute | solution.py:511
  63.5 22.3 %collective-permute-start.12 = (f32[128,128]{1,0:T(8,128)S(1)}, f32[128,128]{1,0:T(8,128)S(1)}, u32[]{:S(2)}, u32[]{:S(2)}) collective-permute-start(f32[128,128]{1,0:T(8,128)S(1)} %row_merge_two.1.lse.first_lse), channel_id=1, source_target_pairs={{0,2},{1,3},{2,0},{3,1},{4,6},{5,7},{6,4},{7,5},{8,10},{9,11},{10,... | collective-permute-start | bytes 196616 | tf_op jit(solution)/shard_map/ppermute | solution.py:511
  65.5 20.4 %collective-permute-start.13 = (f32[128,128]{1,0:T(8,128)S(1)}, f32[128,128]{1,0:T(8,128)S(1)}, u32[]{:S(2)}, u32[]{:S(2)}) collective-permute-start(f32[128,128]{1,0:T(8,128)S(1)} %row_merge_two.1.lse.first_lse), channel_id=1, source_target_pairs={{0,3},{1,0},{2,1},{3,2},{4,7},{5,4},{6,5},{7,6},{8,11},{9,8},{10,9... | collective-permute-start | bytes 196616 | tf_op jit(solution)/shard_map/ppermute | solution.py:511
  67.2 13.1 %copy-start.5 = (s32[1,65536]{1,0:T(1,128)S(1)}, s32[1,65536]{1,0:T(1,128)}, u32[]{:S(2)}) copy-start(s32[1,65536]{1,0:T(1,128)} %order_all.1) | copy-start | bytes 786436
  77.9 7.6 %collective-permute-start.7 = (f32[16,128]{1,0:T(8,128)S(1)}, f32[16,128]{1,0:T(8,128)S(1)}, u32[]{:S(2)}, u32[]{:S(2)}) collective-permute-start(f32[16,128]{1,0:T(8,128)S(1)} %get-tuple-element.28), channel_id=1, source_target_pairs={{0,3},{1,0},{2,1},{3,2},{4,7},{5,4},{6,5},{7,6},{8,11},{9,8},{10,9... | collective-permute-start | bytes 24584 | tf_op jit(solution)/shard_map/ppermute | solution.py:539
  78.3 7.1 %collective-permute-start.8 = (f32[16,128]{1,0:T(8,128)S(1)}, f32[16,128]{1,0:T(8,128)S(1)}, u32[]{:S(2)}, u32[]{:S(2)}) collective-permute-start(f32[16,128]{1,0:T(8,128)S(1)} %get-tuple-element.27), channel_id=1, source_target_pairs={{0,2},{1,3},{2,0},{3,1},{4,6},{5,7},{6,4},{7,5},{8,10},{9,11},{10,... | collective-permute-start | bytes 24584 | tf_op jit(solution)/shard_map/ppermute | solution.py:539
  80.3 5.2 %collective-permute-start.9 = (f32[16,128]{1,0:T(8,128)S(1)}, f32[16,128]{1,0:T(8,128)S(1)}, u32[]{:S(2)}, u32[]{:S(2)}) collective-permute-start(f32[16,128]{1,0:T(8,128)S(1)} %get-tuple-element.26), channel_id=1, source_target_pairs={{0,1},{1,2},{2,3},{3,0},{4,5},{5,6},{6,7},{7,4},{8,9},{9,10},{10,1... | collective-permute-start | bytes 24584 | tf_op jit(solution)/shard_map/ppermute | solution.py:539
  80.3 5.5 %copy-start.4 = (f32[65536]{0:T(1024)S(1)}, f32[65536]{0:T(1024)}, u32[]{:S(2)}) copy-start(f32[65536]{0:T(1024)} %param.14) | copy-start | bytes 786436
  85.5 5.6 %collective-permute-start.11 = (f32[16,128]{1,0:T(8,128)S(1)}, f32[16,128]{1,0:T(8,128)S(1)}, u32[]{:S(2)}, u32[]{:S(2)}) collective-permute-start(f32[16,128]{1,0:T(8,128)S(1)} %col_merge_y.1.refs_0_), channel_id=1, source_target_pairs={{0,32},{32,0},{64,96},{96,64},{128,160},{160,128},{192,224},{224,1... | collective-permute-start | bytes 24584 | tf_op jit(solution)/shard_map/ppermute | solution.py:551
  85.9 16.0 %copy-start.1 = (s32[1,2048]{1,0:T(1,128)S(1)}, s32[1,2048]{1,0:T(1,128)}, u32[]{:S(2)}) copy-start(s32[1,2048]{1,0:T(1,128)} %refs_1_.1) | copy-start | bytes 24580
  85.9 16.0 %copy-start.2 = (f32[2048]{0:T(1024)S(1)}, f32[2048]{0:T(1024)}, u32[]{:S(2)}) copy-start(f32[2048]{0:T(1024)} %param.16) | copy-start | bytes 24580
  85.9 16.0 %copy-start.3 = (f32[2048]{0:T(1024)S(1)}, f32[2048]{0:T(1024)}, u32[]{:S(2)}) copy-start(f32[2048]{0:T(1024)} %param.15) | copy-start | bytes 24580
  91.1 10.8 %collective-permute-start.17 = (f32[256,128]{1,0:T(8,128)S(1)}, f32[256,128]{1,0:T(8,128)S(1)}, u32[]{:S(2)}, u32[]{:S(2)}) collective-permute-start(f32[256,128]{1,0:T(8,128)S(1)} %source_scatter_1.1.refs_7_), channel_id=1, source_target_pairs={{0,4},{1,5},{2,6},{3,7},{4,0},{5,1},{6,2},{7,3},{8,12},{9,13},{10,... | collective-permute-start | bytes 393224 | tf_op jit(solution)/shard_map/ppermute | solution.py:561
  93.0 4.0 %collective-permute-start.14 = (f32[16,128]{1,0:T(8,128)S(1)}, f32[16,128]{1,0:T(8,128)S(1)}, u32[]{:S(2)}, u32[]{:S(2)}) collective-permute-start(f32[16,128]{1,0:T(8,128)S(1)} %col_merge_core.1.refs_0_), channel_id=1, source_target_pairs={{0,64},{32,96},{64,128},{96,160},{128,192},{160,224},{192,0},{224,... | collective-permute-start | bytes 24584 | tf_op jit(solution)/shard_map/ppermute | solution.py:563
  93.1 5.5 %collective-permute-start.15 = (f32[16,128]{1,0:T(8,128)S(1)}, f32[16,128]{1,0:T(8,128)S(1)}, u32[]{:S(2)}, u32[]{:S(2)}) collective-permute-start(f32[16,128]{1,0:T(8,128)S(1)} %col_merge_core.1.refs_0_), channel_id=1, source_target_pairs={{0,128},{32,160},{64,192},{96,224},{128,0},{160,32},{192,64},{224,... | collective-permute-start | bytes 24584 | tf_op jit(solution)/shard_map/ppermute | solution.py:563
  97.0 4.9 %collective-permute-start.16 = (f32[16,128]{1,0:T(8,128)S(1)}, f32[16,128]{1,0:T(8,128)S(1)}, u32[]{:S(2)}, u32[]{:S(2)}) collective-permute-start(f32[16,128]{1,0:T(8,128)S(1)} %col_merge_core.1.refs_0_), channel_id=1, source_target_pairs={{0,192},{32,224},{64,0},{96,32},{128,64},{160,96},{192,128},{224,1... | collective-permute-start | bytes 24584 | tf_op jit(solution)/shard_map/ppermute | solution.py:563
